TPU v7x, 128 devices: a whole 4x4x4 slice. The times are simulated.
128 devices in a mesh: dp: 32 (over z, y, x_lo), tensor: 4 (over x_hi, core).
Axes of the slice: x: 4 (x_hi: 2, x_lo: 2; x = x_hi * 2 + x_lo), y: 4, z: 4, core: 2. Of those that a mesh axis runs over, the one named last changes fastest.
Arguments:
- tokens: bfloat16 [32, 1024, 1024], P('dp', 'tensor'), may hold values from -6 to 6
- doc_starts: int32 [32, 4], P('dp'), may hold values from 0 to 1023, as said below
- cotangent: bfloat16 [32, 1024, 1024], P('dp', 'tensor'), may hold values from -12 to 12
- w_query: bfloat16 [1024, 2048], P(None, 'tensor'), may hold values from -0.1875 to 0.1875
- key_matrix: bfloat16 [1024, 1024], P(None, 'tensor'), may hold values from -0.1875 to 0.1875
- value_matrix: bfloat16 [1024, 1024], P(None, 'tensor'), may hold values from -0.1875 to 0.1875
- w_out: bfloat16 [2048, 1024], P('tensor'), may hold values from -0.75 to 0.75
- w_gate: bfloat16 [1024, 3072], P(None, 'tensor'), may hold values from -0.1875 to 0.1875
- w_up: bfloat16 [1024, 3072], P(None, 'tensor'), may hold values from -0.1875 to 0.1875
- w_down: bfloat16 [3072, 1024], P('tensor'), may hold values from -0.21875 to 0.21875
- gain_attn: float32 [1024], replicated, may hold values from 0.5 to 1.5
- gain_mlp: float32 [1024], replicated, may hold values from 0.5 to 1.5
- gain_query: float32 [128], replicated, may hold values from 0.5 to 1.5
- gain_key: float32 [128], replicated, may hold values from 0.5 to 1.5
Outputs:
- layer_out: bfloat16 [32, 1024, 1024], P('dp', 'tensor')
- grad_tokens: float32 [32, 1024, 1024], P('dp', 'tensor')
- grad_w_query: float32 [1024, 2048], P('dp', 'tensor')
- grad_w_key: float32 [1024, 1024], P('dp', 'tensor')
- grad_w_value: float32 [1024, 1024], P('dp', 'tensor')
- grad_w_out: float32 [2048, 1024], P('tensor', 'dp')
- grad_w_gate: float32 [1024, 3072], P('dp', 'tensor')
- grad_w_up: float32 [1024, 3072], P('dp', 'tensor')
- grad_w_down: float32 [3072, 1024], P('tensor', 'dp')
- grad_gain_attn: float32 [1024], replicated
- grad_gain_mlp: float32 [1024], replicated
- grad_gain_query: float32 [128], replicated
- grad_gain_key: float32 [128], replicated
Inputs may be any that keep to these rules, and one draw needn't show every extreme that they name: `doc_starts`: each row lists the first tokens of 4 documents that tile a sequence of 1024 tokens in order: the first is 0 and they rise strictly. In each sequence one document, at a place drawn from the seed, starts before token 193 and reaches token 831; each other document has at most 64 tokens.
All inputs are finite; a program needn't handle non-finite values.
Results may differ from a plain program's by a relative error of at most 0.03.
Values may be sent and summed in bfloat16 or wider, within the bound.
A program may use at most 128 MiB of HBM per device.

v0:
```python
import jax
import jax.numpy as jnp
from jax import lax
from jax.sharding import PartitionSpec as P

epsilon = 1e-06
rope_base = 1000000.0
masked_fill = -1e30


def rms_scale(values, scale_gain):
    return (
        values * lax.rsqrt(jnp.mean(values * values, axis=-1, keepdims=True) + epsilon) * scale_gain
    )


def doc_layout(starts, token_length):
    place_index = jnp.arange(token_length, dtype=jnp.int32)
    started = place_index[:, None] >= starts[..., None, :]
    doc_index = jnp.sum(started.astype(jnp.int32), axis=-1)
    doc_first = jnp.max(jnp.where(started, starts[..., None, :], 0), axis=-1)
    return (doc_index, place_index - doc_first)


def rope_tables(position, head_width):
    half_width = head_width // 2
    frequency = rope_base ** (-(jnp.arange(half_width, dtype=jnp.float32) * 2.0) / head_width)
    angles = position.astype(jnp.float32)[..., None] * frequency
    return (jnp.cos(angles), jnp.sin(angles))


def rotate(values, cosine_table, sine_table):
    half_width = values.shape[-1] // 2
    first_half = values[..., :half_width]
    second_half = values[..., half_width:]
    cosine_heads = cosine_table[..., None, :]
    sine_heads = sine_table[..., None, :]
    return jnp.concatenate(
        [
            first_half * cosine_heads - second_half * sine_heads,
            second_half * cosine_heads + first_half * sine_heads,
        ],
        axis=-1,
    )


def matrix_product(left_side, right_side):
    return jnp.dot(left_side, right_side, preferred_element_type=jnp.float32)


def outer_rows(left_side, right_side):
    return lax.dot_general(
        left_side, right_side, (((0,), (0,)), ((), ())), preferred_element_type=jnp.float32
    )


def times_transposed(left_side, right_side):
    return lax.dot_general(
        left_side, right_side, (((1,), (1,)), ((), ())), preferred_element_type=jnp.float32
    )


def allowed_mask(doc_seq):
    place_index = jnp.arange(doc_seq.shape[0], dtype=jnp.int32)
    return (doc_seq[:, None] == doc_seq[None, :]) & (place_index[:, None] >= place_index[None, :])


def score_block(query_seq, key_seq, doc_seq):
    token_length, heads_query, head_width = query_seq.shape
    heads_key = key_seq.shape[1]
    grouped_heads = query_seq.reshape(token_length, heads_key, heads_query // heads_key, head_width)
    scores = jnp.einsum(
        "qhgd,khd->hgqk", grouped_heads, key_seq, preferred_element_type=jnp.float32
    ) * head_width ** (-0.5)
    return (grouped_heads, jnp.where(allowed_mask(doc_seq)[None, None], scores, masked_fill))


def attend(bundle):
    query_seq, key_seq, value_seq, doc_seq = bundle
    token_length, heads_query, head_width = query_seq.shape
    grouped_heads, scores = score_block(query_seq, key_seq, doc_seq)
    row_top = jnp.max(scores, axis=-1, keepdims=True)
    weights = jnp.exp(scores - row_top)
    row_total = jnp.sum(weights, axis=-1, keepdims=True)
    probabilities = (weights / row_total).astype(jnp.bfloat16)
    attended = jnp.einsum(
        "hgqk,khd->qhgd", probabilities, value_seq, preferred_element_type=jnp.float32
    )
    return (attended.reshape(token_length, heads_query * head_width), row_top + jnp.log(row_total))


def attend_back(bundle):
    query_seq, key_seq, value_seq, doc_seq, log_total, grad_attended = bundle
    token_length, heads_query, head_width = query_seq.shape
    heads_key = key_seq.shape[1]
    grouped_heads, scores = score_block(query_seq, key_seq, doc_seq)
    probabilities = jnp.exp(scores - log_total)
    grad_grouped = grad_attended.reshape(
        token_length, heads_key, heads_query // heads_key, head_width
    )
    grad_probs = jnp.einsum(
        "qhgd,khd->hgqk", grad_grouped, value_seq, preferred_element_type=jnp.float32
    )
    grad_value = jnp.einsum(
        "hgqk,qhgd->khd",
        probabilities.astype(jnp.bfloat16),
        grad_grouped,
        preferred_element_type=jnp.float32,
    )
    row_inner = jnp.sum(grad_probs * probabilities, axis=-1, keepdims=True)
    grad_scores = (probabilities * (grad_probs - row_inner)).astype(jnp.bfloat16)
    score_scale = head_width ** (-0.5)
    grad_query = (
        jnp.einsum("hgqk,khd->qhgd", grad_scores, key_seq, preferred_element_type=jnp.float32)
        * score_scale
    )
    grad_key = (
        jnp.einsum("hgqk,qhgd->khd", grad_scores, grouped_heads, preferred_element_type=jnp.float32)
        * score_scale
    )
    return (grad_query.reshape(token_length, heads_query, head_width), grad_key, grad_value)


def shards(
    tokens,
    doc_starts,
    cotangent,
    w_query,
    key_matrix,
    value_matrix,
    w_out,
    w_gate,
    w_up,
    w_down,
    gain_attn,
    gain_mlp,
    gain_query,
    gain_key,
):
    seq_count, quarter, model_width = tokens.shape
    head_width = gain_query.shape[0]
    heads_query = w_query.shape[1] // head_width
    heads_key = key_matrix.shape[1] // head_width
    token_length = quarter * lax.axis_size("tensor")
    rows_all = seq_count * token_length
    doc_index, position = doc_layout(doc_starts, token_length)
    cosine_table, sine_table = rope_tables(position, head_width)

    def head_path(raw_values, scale_gain):
        return rotate(rms_scale(raw_values, scale_gain), cosine_table, sine_table)

    inputs = tokens.astype(jnp.float32)
    normed_attn = rms_scale(inputs, gain_attn).astype(jnp.bfloat16)
    gathered_attn = lax.all_gather(normed_attn, "tensor", axis=1, tiled=True).reshape(
        rows_all, model_width
    )
    raw_query = matrix_product(gathered_attn, w_query).reshape(
        seq_count, token_length, heads_query, head_width
    )
    unrotated_key = matrix_product(gathered_attn, key_matrix).reshape(
        seq_count, token_length, heads_key, head_width
    )
    value_seq = (
        matrix_product(gathered_attn, value_matrix)
        .astype(jnp.bfloat16)
        .reshape(seq_count, token_length, heads_key, head_width)
    )
    rotated_query = head_path(raw_query, gain_query).astype(jnp.bfloat16)
    key_rot = head_path(unrotated_key, gain_key).astype(jnp.bfloat16)
    attended, log_total = lax.map(attend, (rotated_query, key_rot, value_seq, doc_index))
    attended_low = attended.astype(jnp.bfloat16).reshape(rows_all, heads_query * head_width)
    attn_part = matrix_product(attended_low, w_out).reshape(seq_count, token_length, model_width)
    attn_share = lax.psum_scatter(
        attn_part.astype(jnp.bfloat16), "tensor", scatter_dimension=1, tiled=True
    ).astype(jnp.float32)
    residual = inputs + attn_share
    normed_mlp = rms_scale(residual, gain_mlp).astype(jnp.bfloat16)
    gathered_mlp = lax.all_gather(normed_mlp, "tensor", axis=1, tiled=True).reshape(
        rows_all, model_width
    )
    gate_rows = matrix_product(gathered_mlp, w_gate)
    up_rows = matrix_product(gathered_mlp, w_up)
    hidden = (jax.nn.silu(gate_rows) * up_rows).astype(jnp.bfloat16)
    mlp_part = matrix_product(hidden, w_down).reshape(seq_count, token_length, model_width)
    mlp_share = lax.psum_scatter(
        mlp_part.astype(jnp.bfloat16), "tensor", scatter_dimension=1, tiled=True
    ).astype(jnp.float32)
    layer_out = (residual + mlp_share).astype(jnp.bfloat16)
    grad_rows = lax.all_gather(cotangent, "tensor", axis=1, tiled=True).reshape(
        rows_all, model_width
    )
    grad_w_down = outer_rows(hidden, grad_rows)
    grad_hidden = times_transposed(grad_rows, w_down)
    sigmoid_rows = jax.nn.sigmoid(gate_rows)
    grad_gate = (
        grad_hidden * up_rows * sigmoid_rows * (1.0 + gate_rows * (1.0 - sigmoid_rows))
    ).astype(jnp.bfloat16)
    grad_up = (grad_hidden * jax.nn.silu(gate_rows)).astype(jnp.bfloat16)
    grad_w_gate = outer_rows(gathered_mlp, grad_gate)
    grad_w_up = outer_rows(gathered_mlp, grad_up)
    grad_normed_mlp = (
        times_transposed(grad_gate, w_gate) + times_transposed(grad_up, w_up)
    ).reshape(seq_count, token_length, model_width)
    grad_mlp_share = lax.psum_scatter(
        grad_normed_mlp.astype(jnp.bfloat16), "tensor", scatter_dimension=1, tiled=True
    ).astype(jnp.float32)
    mlp_norm_back = jax.vjp(rms_scale, residual, gain_mlp)[1]
    grad_resid_norm, grad_gain_mlp = mlp_norm_back(grad_mlp_share)
    grad_residual = cotangent.astype(jnp.float32) + grad_resid_norm
    grad_attn_rows = lax.all_gather(
        grad_residual.astype(jnp.bfloat16), "tensor", axis=1, tiled=True
    ).reshape(rows_all, model_width)
    grad_w_out = outer_rows(attended_low, grad_attn_rows)
    grad_attended = (
        times_transposed(grad_attn_rows, w_out)
        .astype(jnp.bfloat16)
        .reshape(seq_count, token_length, heads_query * head_width)
    )
    grad_query_rot, grad_key_rot, grad_value = lax.map(
        attend_back, (rotated_query, key_rot, value_seq, doc_index, log_total, grad_attended)
    )
    query_back = jax.vjp(head_path, raw_query, gain_query)[1]
    grad_raw_query, grad_gain_query = query_back(grad_query_rot)
    key_back = jax.vjp(head_path, unrotated_key, gain_key)[1]
    grad_raw_key, grad_gain_key = key_back(grad_key_rot)
    grad_query_low = grad_raw_query.astype(jnp.bfloat16).reshape(rows_all, heads_query * head_width)
    grad_key_low = grad_raw_key.astype(jnp.bfloat16).reshape(rows_all, heads_key * head_width)
    grad_value_low = grad_value.astype(jnp.bfloat16).reshape(rows_all, heads_key * head_width)
    grad_w_query = outer_rows(gathered_attn, grad_query_low)
    grad_w_key = outer_rows(gathered_attn, grad_key_low)
    grad_w_value = outer_rows(gathered_attn, grad_value_low)
    grad_normed_attn = (
        times_transposed(grad_query_low, w_query)
        + times_transposed(grad_key_low, key_matrix)
        + times_transposed(grad_value_low, value_matrix)
    ).reshape(seq_count, token_length, model_width)
    grad_attn_share = lax.psum_scatter(
        grad_normed_attn.astype(jnp.bfloat16), "tensor", scatter_dimension=1, tiled=True
    ).astype(jnp.float32)
    attn_norm_back = jax.vjp(rms_scale, inputs, gain_attn)[1]
    grad_inputs_norm, grad_gain_attn = attn_norm_back(grad_attn_share)
    grad_tokens = grad_residual + grad_inputs_norm
    summed_gains = lax.psum(
        (grad_gain_attn, grad_gain_mlp, grad_gain_query, grad_gain_key), ("dp", "tensor")
    )
    summed_weights = (
        lax.psum_scatter(
            grad_w_query.astype(jnp.bfloat16), "dp", scatter_dimension=0, tiled=True
        ).astype(jnp.float32),
        lax.psum_scatter(
            grad_w_key.astype(jnp.bfloat16), "dp", scatter_dimension=0, tiled=True
        ).astype(jnp.float32),
        lax.psum_scatter(
            grad_w_value.astype(jnp.bfloat16), "dp", scatter_dimension=0, tiled=True
        ).astype(jnp.float32),
        lax.psum_scatter(
            grad_w_out.astype(jnp.bfloat16), "dp", scatter_dimension=1, tiled=True
        ).astype(jnp.float32),
        lax.psum_scatter(
            grad_w_gate.astype(jnp.bfloat16), "dp", scatter_dimension=0, tiled=True
        ).astype(jnp.float32),
        lax.psum_scatter(
            grad_w_up.astype(jnp.bfloat16), "dp", scatter_dimension=0, tiled=True
        ).astype(jnp.float32),
        lax.psum_scatter(
            grad_w_down.astype(jnp.bfloat16), "dp", scatter_dimension=1, tiled=True
        ).astype(jnp.float32),
    )
    return (
        layer_out,
        grad_tokens,
        summed_weights[0],
        summed_weights[1],
        summed_weights[2],
        summed_weights[3],
        summed_weights[4],
        summed_weights[5],
        summed_weights[6],
        summed_gains[0],
        summed_gains[1],
        summed_gains[2],
        summed_gains[3],
    )


def solution(mesh):
    in_specs = (
        P("dp", "tensor", None),
        P("dp", None),
        P("dp", "tensor", None),
        P(None, "tensor"),
        P(None, "tensor"),
        P(None, "tensor"),
        P("tensor", None),
        P(None, "tensor"),
        P(None, "tensor"),
        P("tensor", None),
        P(),
        P(),
        P(),
        P(),
    )
    out_specs = (
        P("dp", "tensor", None),
        P("dp", "tensor", None),
        P("dp", "tensor"),
        P("dp", "tensor"),
        P("dp", "tensor"),
        P("tensor", "dp"),
        P("dp", "tensor"),
        P("dp", "tensor"),
        P("tensor", "dp"),
        P(),
        P(),
        P(),
        P(),
    )
    return jax.shard_map(shards, mesh=mesh, in_specs=in_specs, out_specs=out_specs, check_vma=False)
```

profile of v0, /device:TPU:6, one launch (start us, length us, event | category | flops | bytes accessed | tf_op | source)
XLA Modules:
  0.0 1508.4 jit_solution(5034959191077610279)
XLA Ops:
  14.7 23.5 %all-gather.5.cloned.1.call-done = bf16[1,1024,1024]{2,1,0:T(8,128)(2,1)} async-done(((bf16[1,256,1024]{2,1,0:T(8,128)(2,1)}), bf16[1,1024,1024]{2,1,0:T(8,128)(2,1)}) %all-gather.5.cloned.1.call-update) | async-done | bytes 2097168 | tf_op jit(solution)/shard_map/all_gather | solution.py:154
  43.3 3.5 fusion.35
  57.9 8.5 fusion.101
  66.5 8.2 fusion.3
  75.4 7.8 fusion.51
  87.0 37.9 %reduce-scatter.12.cloned.1.call-done = bf16[1,256,1024]{2,1,0:T(8,128)(2,1)} async-done(((bf16[1,1024,1024]{2,1,0:T(8,128)(2,1)}), bf16[1,256,1024]{2,1,0:T(8,128)(2,1)}) %reduce-scatter.12.cloned.1.call-update) | async-done | bytes 524304 | tf_op jit(solution)/shard_map/reduce_scatter | solution.py:173
  128.9 25.6 %all-gather.7.cloned.1.call-done = bf16[1,1024,1024]{2,1,0:T(8,128)(2,1)} async-done(((bf16[1,256,1024]{2,1,0:T(8,128)(2,1)}), bf16[1,1024,1024]{2,1,0:T(8,128)(2,1)}) %all-gather.7.cloned.1.call-update) | async-done | bytes 2097168 | tf_op jit(solution)/shard_map/all_gather | solution.py:178
  154.5 5.7 fusion.25
  160.2 3.4 fusion.27
  163.6 18.6 %all-gather.9.cloned.1.call-done = bf16[1,1024,1024]{2,1,0:T(8,128)(2,1)} async-done(((bf16[1,256,1024]{2,1,0:T(8,128)(2,1)}), bf16[1,1024,1024]{2,1,0:T(8,128)(2,1)}) %all-gather.9.cloned.1.call-update) | async-done | bytes 2097168 | tf_op jit(solution)/shard_map/all_gather | solution.py:189
  182.2 7.2 multiply_convert_fusion
  195.3 37.9 %reduce-scatter.16.cloned.1.call-done = bf16[1,256,1024]{2,1,0:T(8,128)(2,1)} async-done(((bf16[1,1024,1024]{2,1,0:T(8,128)(2,1)}), bf16[1,256,1024]{2,1,0:T(8,128)(2,1)}) %reduce-scatter.16.cloned.1.call-update) | async-done | bytes 524304 | tf_op jit(solution)/shard_map/reduce_scatter | solution.py:204
  237.6 5.1 fusion.47
  242.8 5.1 fusion.44
  247.9 5.5 fusion.41
  253.7 10.1 all-gather.11.cloned.1.call-done
  266.9 9.2 fusion.66
  278.5 10.5 fusion
  289.0 8.4 fusion.2
  300.7 3.4 fusion.65
  314.0 4.2 fusion.58
  318.4 5.2 convolution_multiply_fusion
  336.6 4.5 convert_bitcast_fusion
  341.2 84.9 %reduce-scatter.32.cloned.1.call-done = bf16[768,32]{0,1:T(8,128)(2,1)} async-done(((bf16[768,1024]{0,1:T(8,128)(2,1)}), bf16[768,32]{0,1:T(8,128)(2,1)}) %reduce-scatter.32.cloned.1.call-update) | async-done | bytes 49168 | tf_op jit(solution)/shard_map/reduce_scatter | solution.py:265
  427.6 160.7 %reduce-scatter.30.cloned.1.call-done = bf16[32,768]{1,0:T(8,128)(2,1)} async-done(((bf16[1024,768]{1,0:T(8,128)(2,1)}), bf16[32,768]{1,0:T(8,128)(2,1)}) %reduce-scatter.30.cloned.1.call-update) | async-done | bytes 49168 | tf_op jit(solution)/shard_map/reduce_scatter | solution.py:262
  589.8 160.6 %reduce-scatter.28.cloned.1.call-done = bf16[32,768]{1,0:T(8,128)(2,1)} async-done(((bf16[1024,768]{1,0:T(8,128)(2,1)}), bf16[32,768]{1,0:T(8,128)(2,1)}) %reduce-scatter.28.cloned.1.call-update) | async-done | bytes 49168 | tf_op jit(solution)/shard_map/reduce_scatter | solution.py:259
  751.9 157.8 %reduce-scatter.24.cloned.1.call-done = bf16[32,256]{1,0:T(8,128)(2,1)} async-done(((bf16[1024,256]{1,0:T(8,128)(2,1)}), bf16[32,256]{1,0:T(8,128)(2,1)}) %reduce-scatter.24.cloned.1.call-update) | async-done | bytes 16400 | tf_op jit(solution)/shard_map/reduce_scatter | solution.py:253
  911.0 157.6 %reduce-scatter.22.cloned.1.call-done = bf16[32,256]{1,0:T(8,128)(2,1)} async-done(((bf16[1024,256]{1,0:T(8,128)(2,1)}), bf16[32,256]{1,0:T(8,128)(2,1)}) %reduce-scatter.22.cloned.1.call-update) | async-done | bytes 16400 | tf_op jit(solution)/shard_map/reduce_scatter | solution.py:250
  1069.9 158.4 %reduce-scatter.26.cloned.1.call-done = bf16[512,32]{0,1:T(8,128)(2,1)} async-done(((bf16[512,1024]{0,1:T(8,128)(2,1)}), bf16[512,32]{0,1:T(8,128)(2,1)}) %reduce-scatter.26.cloned.1.call-update) | async-done | bytes 32784 | tf_op jit(solution)/shard_map/reduce_scatter | solution.py:256
  1229.7 158.6 %reduce-scatter.20.cloned.1.call-done = bf16[32,512]{1,0:T(8,128)(2,1)} async-done(((bf16[1024,512]{1,0:T(8,128)(2,1)}), bf16[32,512]{1,0:T(8,128)(2,1)}) %reduce-scatter.20.cloned.1.call-update) | async-done | bytes 32784 | tf_op jit(solution)/shard_map/reduce_scatter | solution.py:247
  1389.7 39.1 %reduce-scatter.18.cloned.1.call-done = bf16[1,256,1024]{2,1,0:T(8,128)(2,1)} async-done(((bf16[1,1024,1024]{2,1,0:T(8,128)(2,1)}), bf16[1,256,1024]{2,1,0:T(8,128)(2,1)}) %reduce-scatter.18.cloned.1.call-update) | async-done | bytes 524304 | tf_op jit(solution)/shard_map/reduce_scatter | solution.py:237
  1430.3 68.0 %all-reduce.4 = (f32[1024]{0:T(1024)}, f32[1024]{0:T(1024)}, f32[128]{0:T(128)}, f32[128]{0:T(128)}) all-reduce(f32[1024]{0:T(1024)S(1)} %get-tuple-element.70, f32[1024]{0:T(1024)S(1)} %copy-done.50, f32[128]{0:T(128)S(1)} %get-tuple-element.54, f32[128]{0:T(128)S(1)} %get-tuple-element.56), channel_id=1, replica_groups=mesh['dp'=32,'tensor'=4] {'dp','tensor'}, use_global_device_ids=true, to_apply=%region_25.26 | all-reduce | flops 2304 | bytes 18432 | tf_op jit(solution)/shard_map/psum | solution.py:243
  (230 shorter events, 88.7 us)
Async XLA Ops:
  7.2 175.0 %copy-start = (bf16[768,1024]{1,0:T(8,128)(2,1)S(1)}, bf16[768,1024]{1,0:T(8,128)(2,1)}, u32[]{:S(2)}) copy-start(bf16[768,1024]{1,0:T(8,128)(2,1)} %param.23) | copy-start | bytes 4718596
  7.2 31.0 %all-gather.5.cloned.1.call-start = ((), (), s32[]{:S(2)}) async-start(), calls=%async_computation.11 | async-start | bytes 2621440 | tf_op jit(solution)/shard_map/all_gather | solution.py:154
  10.7 114.2 %reduce-scatter.12.cloned.1.call-start = ((), (), s32[]{:S(2)}) async-start(), calls=%async_computation.12 | async-start | bytes 2621440 | tf_op jit(solution)/shard_map/reduce_scatter | solution.py:173
  11.9 36.1 %copy-start.14 = (f32[1024,64]{0,1:T(8,128)}, f32[1024,64]{0,1:T(8,128)S(1)}, u32[]{:S(2)}) copy-start(f32[1024,64]{0,1:T(8,128)S(1)} %get-tuple-element.91) | copy-start | bytes 786436
  12.1 42.9 %copy-start.9 = (f32[1024,64]{1,0:T(8,128)}, f32[1024,64]{1,0:T(8,128)S(1)}, u32[]{:S(2)}) copy-start(f32[1024,64]{1,0:T(8,128)S(1)} %copy.78) | copy-start | bytes 786436
  86.9 38.0 %copy-start.4 = (bf16[1,256,1024]{2,1,0:T(8,128)(2,1)S(1)}, bf16[1,256,1024]{2,1,0:T(8,128)(2,1)}, u32[]{:S(2)}) copy-start(bf16[1,256,1024]{2,1,0:T(8,128)(2,1)} %param.14) | copy-start | bytes 1572868
  86.9 39.3 %copy-start.45 = (f32[1024]{0:T(1024)S(1)}, f32[1024]{0:T(1024)}, u32[]{:S(2)}) copy-start(f32[1024]{0:T(1024)} %param.25) | copy-start | bytes 12292
  87.0 67.5 %all-gather.7.cloned.1.call-start = ((), (), s32[]{:S(2)}) async-start(), calls=%async_computation.13 | async-start | bytes 2621440 | tf_op jit(solution)/shard_map/all_gather | solution.py:178
  126.2 109.1 %copy-start.48 = (f32[256]{0:T(256)}, f32[256]{0:T(256)S(1)}, u32[]{:S(2)}) copy-start(f32[256]{0:T(256)S(1)} %fusion.96) | copy-start | bytes 3076
  128.3 53.9 %all-gather.9.cloned.1.call-start = ((), (), s32[]{:S(2)}) async-start(), calls=%async_computation.15 | async-start | bytes 2621440 | tf_op jit(solution)/shard_map/all_gather | solution.py:189
  128.9 104.3 %reduce-scatter.16.cloned.1.call-start = ((), (), s32[]{:S(2)}) async-start(), calls=%async_computation.16 | async-start | bytes 2621440 | tf_op jit(solution)/shard_map/reduce_scatter | solution.py:204
  195.2 37.9 %copy-start.7 = (bf16[1,256,1024]{2,1,0:T(8,128)(2,1)S(1)}, bf16[1,256,1024]{2,1,0:T(8,128)(2,1)}, u32[]{:S(2)}) copy-start(bf16[1,256,1024]{2,1,0:T(8,128)(2,1)} %reduce-scatter.12.cloned.1.call-done) | copy-start | bytes 1572868
  195.2 40.1 %copy-start.12 = (bf16[1,256,1024]{2,1,0:T(8,128)(2,1)S(1)}, bf16[1,256,1024]{2,1,0:T(8,128)(2,1)}, u32[]{:S(2)}) copy-start(bf16[1,256,1024]{2,1,0:T(8,128)(2,1)} %param.16) | copy-start | bytes 1572868
  195.2 68.5 %all-gather.11.cloned.1.call-start = ((), (), s32[]{:S(2)}) async-start(), calls=%async_computation.17 | async-start | bytes 2621440 | tf_op jit(solution)/shard_map/all_gather | solution.py:210
  237.6 188.6 %reduce-scatter.32.cloned.1.call-start = ((), (), s32[]{:S(2)}) async-start(), calls=%async_computation.25 | async-start | bytes 1622016 | tf_op jit(solution)/shard_map/reduce_scatter | solution.py:265
  242.7 345.6 %reduce-scatter.30.cloned.1.call-start = ((), (), s32[]{:S(2)}) async-start(), calls=%async_computation.24 | async-start | bytes 1622016 | tf_op jit(solution)/shard_map/reduce_scatter | solution.py:262
  247.9 502.5 %reduce-scatter.28.cloned.1.call-start = ((), (), s32[]{:S(2)}) async-start(), calls=%async_computation.23 | async-start | bytes 1622016 | tf_op jit(solution)/shard_map/reduce_scatter | solution.py:259
  253.4 656.2 %reduce-scatter.24.cloned.1.call-start = ((), (), s32[]{:S(2)}) async-start(), calls=%async_computation.21 | async-start | bytes 540672 | tf_op jit(solution)/shard_map/reduce_scatter | solution.py:253
  289.0 11.7 copy-start.24
  304.1 764.5 %reduce-scatter.22.cloned.1.call-start = ((), (), s32[]{:S(2)}) async-start(), calls=%async_computation.20 | async-start | bytes 540672 | tf_op jit(solution)/shard_map/reduce_scatter | solution.py:250
  314.0 914.3 %reduce-scatter.26.cloned.1.call-start = ((), (), s32[]{:S(2)}) async-start(), calls=%async_computation.22 | async-start | bytes 1081344 | tf_op jit(solution)/shard_map/reduce_scatter | solution.py:256
  318.3 1070.0 %reduce-scatter.20.cloned.1.call-start = ((), (), s32[]{:S(2)}) async-start(), calls=%async_computation.19 | async-start | bytes 1081344 | tf_op jit(solution)/shard_map/reduce_scatter | solution.py:247
  330.0 1098.8 %reduce-scatter.18.cloned.1.call-start = ((), (), s32[]{:S(2)}) async-start(), calls=%async_computation.18 | async-start | bytes 2621440 | tf_op jit(solution)/shard_map/reduce_scatter | solution.py:237
  336.4 1162.0 %reduce-scatter.14.cloned.1.call-start = ((), (), s32[]{:S(2)}) async-start(), calls=%async_computation.14 | async-start | bytes 2621440 | tf_op jit(solution)/shard_map/reduce_scatter | solution.py:185
  341.2 1087.6 %copy-start.47 = (f32[1024]{0:T(1024)S(1)}, f32[1024]{0:T(1024)}, u32[]{:S(2)}) copy-start(f32[1024]{0:T(1024)} %param.24) | copy-start | bytes 12292
  341.2 1087.6 %copy-start.52 = (f32[256]{0:T(256)S(1)}, f32[256]{0:T(256)}, u32[]{:S(2)}) copy-start(f32[256]{0:T(256)} %copy-done.51) | copy-start | bytes 3076
  341.2 1089.2 %copy-start.50 = (f32[1024]{0:T(1024)S(1)}, f32[1024]{0:T(1024)}, u32[]{:S(2)}) copy-start(f32[1024]{0:T(1024)} %get-tuple-element.68) | copy-start | bytes 12292
  341.2 1157.2 %copy-start.54 = (f32[256]{0:T(256)S(1)}, f32[256]{0:T(256)}, u32[]{:S(2)}) copy-start(f32[256]{0:T(256)} %copy-done.53) | copy-start | bytes 3076
  341.2 1157.3 %copy-start.13 = (bf16[1,256,1024]{2,1,0:T(8,128)(2,1)S(1)}, bf16[1,256,1024]{2,1,0:T(8,128)(2,1)}, u32[]{:S(2)}) copy-start(bf16[1,256,1024]{2,1,0:T(8,128)(2,1)} %param.16) | copy-start | bytes 1572868
  341.2 1157.3 %copy-start.46 = (f32[1024]{0:T(1024)S(1)}, f32[1024]{0:T(1024)}, u32[]{:S(2)}) copy-start(f32[1024]{0:T(1024)} %param.25) | copy-start | bytes 12292
  341.2 1157.2 %copy-start.49 = (f32[256]{0:T(256)S(1)}, f32[256]{0:T(256)}, u32[]{:S(2)}) copy-start(f32[256]{0:T(256)} %copy-done.48) | copy-start | bytes 3076
  341.2 1157.2 %copy-start.56 = (f32[256]{0:T(256)S(1)}, f32[256]{0:T(256)}, u32[]{:S(2)}) copy-start(f32[256]{0:T(256)} %copy-done.55) | copy-start | bytes 3076
  (53 other events, 204.8 us)
Sparse Core Ops, SparseCore 0:
  10.8 27.3 all-gather.4
  87.1 37.7 reduce-scatter.11
  128.4 26.0 all-gather.6
  156.1 26.0 all-gather.8
  195.4 37.7 reduce-scatter.15
  237.7 26.0 all-gather.10
  266.1 159.9 reduce-scatter.31
  428.6 159.6 reduce-scatter.29
  590.7 159.6 reduce-scatter.27
  752.7 156.9 reduce-scatter.23
  912.0 156.5 reduce-scatter.21
  1070.9 157.3 reduce-scatter.25
  1230.7 157.6 reduce-scatter.19
  1391.0 37.7 reduce-scatter.17
  1431.3 37.9 reduce-scatter.13
where the time goes:
time: 1520 us; the launch traced here: 1510 us
  waiting for transfers between devices  1230 us (81%)
  matrix products  116 us (8%)
  blocking collectives  68 us (4%)
  other arithmetic  54.5 us (4%)
  local copies, waits for them, and re-layouts  21.9 us (1%)
    reduce_scatter x1, waiting for transfers between devices, shards(): lax.psum_scatter(grad_w_up.astype(jnp.bfloat16), 'dp', scatter_dimension=...  161 us
    reduce_scatter x1, waiting for transfers between devices, shards(): lax.psum_scatter(grad_w_gate.astype(jnp.bfloat16), 'dp', scatter_dimensio...  161 us
    reduce_scatter x1, waiting for transfers between devices, shards(): lax.psum_scatter(grad_w_query.astype(jnp.bfloat16), 'dp', scatter_dimensi...  159 us
    reduce_scatter x1, waiting for transfers between devices, shards(): lax.psum_scatter(grad_w_out.astype(jnp.bfloat16), 'dp', scatter_dimension...  158 us
    reduce_scatter x1, waiting for transfers between devices, shards(): lax.psum_scatter(grad_w_value.astype(jnp.bfloat16), 'dp', scatter_dimensi...  158 us
    reduce_scatter x1, waiting for transfers between devices, shards(): lax.psum_scatter(grad_w_key.astype(jnp.bfloat16), 'dp', scatter_dimension...  158 us
    reduce_scatter x1, waiting for transfers between devices, shards(): lax.psum_scatter(grad_w_down.astype(jnp.bfloat16), 'dp', scatter_dimensio...  84.9 us
    psum x1, blocking collectives, shards(): lax.psum((grad_gain_attn, grad_gain_mlp, grad_gain_query, grad_gain_key),...  68 us
  transfers between devices with their start and end apart: 15, of which 14 were waited for; matrix products, arithmetic and copies ran while one was open for 7% of the time, Pallas kernels for 0%

commit v1 on v0

--- a/solution.py
+++ b/solution.py
@@ -1,7 +1,165 @@
 import jax
 import jax.numpy as jnp
 from jax import lax
+from jax.experimental import pallas as pl
+from jax.experimental.pallas import tpu as pltpu
 from jax.sharding import PartitionSpec as P
+
+MESH = pl.DeviceIdType.MESH
+STREAMS = ((0, 1024), (1024, 1024), (2048, 896), (2944, 896))
+ORDERS = (("y1", "y2", "z1", "z2"), ("y2", "y1", "z2", "z1"), ("z1", "z2", "y1", "y2"), ("z2", "z1", "y2", "y1"))
+GAIN_ORDER = ("core", "y1", "y2", "z1", "z2", "x", "far")
+
+
+class Place:
+    def __init__(self):
+        dp = lax.axis_index("dp")
+        tensor = lax.axis_index("tensor")
+        self.z, self.y, self.x = dp // 8, (dp // 2) % 4, dp % 2
+        self.far, self.core = tensor // 2, tensor % 2
+
+    def near(self, name):
+        value = self.y if name[0] == "y" else self.z
+        return value + 1 - 2 * (value % 2) if name[1] == "1" else 3 - value
+
+    def device(self, name):
+        z, y, x, far, core = self.z, self.y, self.x, self.far, self.core
+        if name[0] == "y":
+            y = self.near(name)
+        elif name[0] == "z":
+            z = self.near(name)
+        elif name == "x":
+            x = 1 - x
+        elif name == "far":
+            far = 1 - far
+        else:
+            core = 1 - core
+        return ((z * 4 + y) * 2 + x, far * 2 + core)
+
+
+def remote(src, dst, sems, index, device):
+    copy = pltpu.make_async_remote_copy(
+        src_ref=src,
+        dst_ref=dst,
+        send_sem=sems.at[0, index],
+        recv_sem=sems.at[1, index],
+        device_id=device,
+        device_id_type=MESH,
+    )
+    copy.start()
+    return copy
+
+
+def sum_kernel(grads, gains, out, gains_out, *scratch):
+    halves = scratch[:20]
+    gain_parts, sems, gain_sems = scratch[20:]
+    place = Place()
+    barrier = pltpu.get_barrier_semaphore()
+    for name in GAIN_ORDER:
+        pl.semaphore_signal(barrier, inc=1, device_id=place.device(name), device_id_type=MESH)
+    pl.semaphore_wait(barrier, len(GAIN_ORDER))
+
+    def piece(stream, ref, axis, at):
+        first, width = STREAMS[stream]
+        columns = pl.ds(first, width)
+        return ref.at[:, at, :, :, columns] if axis == "y" else ref.at[at, :, :, :, columns]
+
+    def begin(stream, phase):
+        order = ORDERS[stream]
+        bufs = halves[stream * 5 : stream * 5 + 5]
+        base = stream * 7
+        if phase == 4:
+            return [remote(bufs[3].at[1 - place.x], bufs[4], sems, base + 6, place.device("x"))]
+        name = order[phase]
+        partner = place.device(name)
+        if phase in (1, 3):
+            source = bufs[phase - 1].at[1]
+            return [remote(source, bufs[phase], sems, base + (2 if phase == 1 else 5), partner)]
+        there = place.near(name)
+        other = place_other(order[phase + 1], there)
+        copies = []
+        for j, at in enumerate((there, other)):
+            source = piece(stream, grads, name[0], at) if phase == 0 else bufs[1].at[at]
+            copies.append(remote(source, bufs[phase].at[j], sems, base + (j if phase == 0 else 3 + j), partner))
+        return copies
+
+    def place_other(name, value):
+        return value + 1 - 2 * (value % 2) if name[1] == "1" else 3 - value
+
+    def finish(stream, phase, copies):
+        order = ORDERS[stream]
+        bufs = halves[stream * 5 : stream * 5 + 5]
+        for copy in copies:
+            copy.wait_recv()
+        first, width = STREAMS[stream]
+        if phase == 4:
+            out[:, first : first + width] = bufs[4][...].astype(jnp.float32) + bufs[3][place.x].astype(jnp.float32)
+        elif phase in (1, 3):
+            bufs[phase][...] += bufs[phase - 1][0]
+        else:
+            name = order[phase]
+            mine = place.y if name[0] == "y" else place.z
+            for j, at in enumerate((mine, place_other(order[phase + 1], mine))):
+                if phase == 0:
+                    for k in range(4):
+                        kept = grads[k, at, :, :, first : first + width] if name[0] == "y" else grads[at, k, :, :, first : first + width]
+                        bufs[0][j, k] += kept
+                else:
+                    bufs[2][j] += bufs[1][at]
+
+    started = []
+    flying = [begin(stream, 0) for stream in range(4)]
+    gain_parts[0] = gains[...]
+    gain_copies = [remote(gain_parts.at[0], gain_parts.at[7], gain_sems, 0, place.device(GAIN_ORDER[0]))]
+    for phase in range(5):
+        for stream in range(4):
+            finish(stream, phase, flying[stream])
+            started += flying[stream]
+            if phase < 4:
+                flying[stream] = begin(stream, phase + 1)
+        for step in ((0, 1), (2,), (3,), (4,), (5, 6))[phase]:
+            gain_copies[step].wait_recv()
+            total = gain_parts[step] + gain_parts[7 + step]
+            if step < 6:
+                gain_parts[step + 1] = total
+                gain_copies.append(
+                    remote(
+                        gain_parts.at[step + 1],
+                        gain_parts.at[8 + step],
+                        gain_sems,
+                        step + 1,
+                        place.device(GAIN_ORDER[step + 1]),
+                    )
+                )
+            else:
+                gains_out[...] = total
+    for copy in started + gain_copies:
+        copy.wait_send()
+
+
+def sum_gradients(grads, gains):
+    columns = grads.shape[1]
+    scratch = []
+    for first, width in STREAMS:
+        for lead in ((2, 4, 2), (4, 2), (2, 2), (2,), ()):
+            scratch.append(pltpu.VMEM((*lead, 32, width), jnp.bfloat16))
+    scratch.append(pltpu.VMEM((14, *gains.shape), jnp.float32))
+    scratch.append(pltpu.SemaphoreType.DMA((2, 28)))
+    scratch.append(pltpu.SemaphoreType.DMA((2, 7)))
+    return pl.pallas_call(
+        sum_kernel,
+        out_shape=(
+            jax.ShapeDtypeStruct((32, columns), jnp.float32),
+            jax.ShapeDtypeStruct(gains.shape, jnp.float32),
+        ),
+        in_specs=[pl.BlockSpec(memory_space=pltpu.VMEM)] * 2,
+        out_specs=(pl.BlockSpec(memory_space=pltpu.VMEM),) * 2,
+        scratch_shapes=scratch,
+        compiler_params=pltpu.CompilerParams(
+            collective_id=0, has_side_effects=True, vmem_limit_bytes=48 * 2**20
+        ),
+        name="sum_gradients",
+    )(grads.reshape(4, 4, 2, 32, columns), gains)
 
 epsilon = 1e-06
 rope_base = 1000000.0
@@ -189,7 +347,7 @@
     grad_rows = lax.all_gather(cotangent, "tensor", axis=1, tiled=True).reshape(
         rows_all, model_width
     )
-    grad_w_down = outer_rows(hidden, grad_rows)
+    grad_w_down = outer_rows(grad_rows, hidden)
     grad_hidden = times_transposed(grad_rows, w_down)
     sigmoid_rows = jax.nn.sigmoid(gate_rows)
     grad_gate = (
@@ -210,7 +368,7 @@
     grad_attn_rows = lax.all_gather(
         grad_residual.astype(jnp.bfloat16), "tensor", axis=1, tiled=True
     ).reshape(rows_all, model_width)
-    grad_w_out = outer_rows(attended_low, grad_attn_rows)
+    grad_w_out = outer_rows(grad_attn_rows, attended_low)
     grad_attended = (
         times_transposed(grad_attn_rows, w_out)
         .astype(jnp.bfloat16)
@@ -240,46 +398,28 @@
     attn_norm_back = jax.vjp(rms_scale, inputs, gain_attn)[1]
     grad_inputs_norm, grad_gain_attn = attn_norm_back(grad_attn_share)
     grad_tokens = grad_residual + grad_inputs_norm
-    summed_gains = lax.psum(
-        (grad_gain_attn, grad_gain_mlp, grad_gain_query, grad_gain_key), ("dp", "tensor")
-    )
-    summed_weights = (
-        lax.psum_scatter(
-            grad_w_query.astype(jnp.bfloat16), "dp", scatter_dimension=0, tiled=True
-        ).astype(jnp.float32),
-        lax.psum_scatter(
-            grad_w_key.astype(jnp.bfloat16), "dp", scatter_dimension=0, tiled=True
-        ).astype(jnp.float32),
-        lax.psum_scatter(
-            grad_w_value.astype(jnp.bfloat16), "dp", scatter_dimension=0, tiled=True
-        ).astype(jnp.float32),
-        lax.psum_scatter(
-            grad_w_out.astype(jnp.bfloat16), "dp", scatter_dimension=1, tiled=True
-        ).astype(jnp.float32),
-        lax.psum_scatter(
-            grad_w_gate.astype(jnp.bfloat16), "dp", scatter_dimension=0, tiled=True
-        ).astype(jnp.float32),
-        lax.psum_scatter(
-            grad_w_up.astype(jnp.bfloat16), "dp", scatter_dimension=0, tiled=True
-        ).astype(jnp.float32),
-        lax.psum_scatter(
-            grad_w_down.astype(jnp.bfloat16), "dp", scatter_dimension=1, tiled=True
-        ).astype(jnp.float32),
-    )
+    all_grads = jnp.concatenate(
+        [grad_w_query, grad_w_key, grad_w_value, grad_w_out, grad_w_gate, grad_w_up, grad_w_down], axis=1
+    ).astype(jnp.bfloat16)
+    all_gains = jnp.concatenate(
+        [grad_gain_attn, grad_gain_mlp, grad_gain_query, grad_gain_key, jnp.zeros((6 * 128,), jnp.float32)]
+    ).reshape(24, 128)
+    summed, gain_sums = sum_gradients(all_grads, all_gains)
+    gain_sums = gain_sums.reshape(-1)
     return (
         layer_out,
         grad_tokens,
-        summed_weights[0],
-        summed_weights[1],
-        summed_weights[2],
-        summed_weights[3],
-        summed_weights[4],
-        summed_weights[5],
-        summed_weights[6],
-        summed_gains[0],
-        summed_gains[1],
-        summed_gains[2],
-        summed_gains[3],
+        summed[:, :512],
+        summed[:, 512:768],
+        summed[:, 768:1024],
+        summed[:, 1024:1536].T,
+        summed[:, 1536:2304],
+        summed[:, 2304:3072],
+        summed[:, 3072:].T,
+        gain_sums[:1024],
+        gain_sums[1024:2048],
+        gain_sums[2048:2176],
+        gain_sums[2176:2304],
     )
 
 

time: 1520 us -> 455 us (0.30)
  waiting for transfers between devices: 1230 us -> 170 us
  blocking collectives: 68 us -> 0 us
  Pallas kernels: 0 us -> 66.2 us
  local copies, waits for them, and re-layouts: 21.9 us -> 37.2 us
    reduce_scatter x7 -> x0, waiting for transfers between devices: 1040 us -> none  [the longest x1 161 us: shards(): lax.psum_scatter(grad_w_up.astype(jnp.bfloat16), 'dp', scatter_dimension=...]
    psum x1 -> x0, blocking collectives: 68 us -> none  [shards(): lax.psum((grad_gain_attn, grad_gain_mlp, grad_gain_query, grad_gain_key),...]
    pallas_call x0 -> x1, Pallas kernels: none -> 66.2 us  [sum_gradients(): pl.pallas_call(sum_kernel, out_shape=(jax.ShapeDtypeStruct((32, columns),...]
    reduce_scatter x1, waiting for transfers between devices: 39.1 us -> 0.01 us  [shards(): lax.psum_scatter(grad_normed_attn.astype(jnp.bfloat16), 'tensor', scatter...]
    all_gather x1, waiting for transfers between devices: 10.1 us -> 26.1 us  [shards(): lax.all_gather(grad_residual.astype(jnp.bfloat16), 'tensor', axis=1, tile...]
  transfers between devices with their start and end apart: 15 -> 8, of which waited for: 14 -> 6; matrix products, arithmetic and copies ran while one was open for 7% -> 14% of each run, Pallas kernels for 0% -> 15%
where the time goes in v1:
time: 455 us; the launch traced here: 448 us
  waiting for transfers between devices  170 us (37%)
  matrix products  112 us (25%)
  Pallas kernels  66.2 us (15%)
  other arithmetic  46.1 us (10%)
  local copies, waits for them, and re-layouts  37.2 us (8%)
  between operations  15.5 us (3%)
    pallas_call x1, Pallas kernels, sum_gradients(): pl.pallas_call(sum_kernel, out_shape=(jax.ShapeDtypeStruct((32, columns),...  66.2 us
    reduce_scatter x1, waiting for transfers between devices, shards(): lax.psum_scatter(attn_part.astype(jnp.bfloat16), 'tensor', scatter_dimens...  37.9 us
    reduce_scatter x1, waiting for transfers between devices, shards(): lax.psum_scatter(grad_normed_mlp.astype(jnp.bfloat16), 'tensor', scatter_...  37.9 us
    all_gather x1, waiting for transfers between devices, shards(): lax.all_gather(grad_residual.astype(jnp.bfloat16), 'tensor', axis=1, tile...  26.1 us
    all_gather x1, waiting for transfers between devices, shards(): lax.all_gather(normed_mlp, 'tensor', axis=1, tiled=True)  25.6 us
    all_gather x1, waiting for transfers between devices, shards(): lax.all_gather(normed_attn, 'tensor', axis=1, tiled=True)  23.5 us
    dot_general x7, matrix products, outer_rows(): lax.dot_general(left_side, right_side, (((0,), (0,)), ((), ())), preferre...  23.2 us
    dot_general x7, matrix products, matrix_product(): return jnp.dot(left_side, right_side, preferred_element_type=jnp.float32)  22.9 us
  transfers between devices with their start and end apart: 8, of which 6 were waited for; matrix products, arithmetic and copies ran while one was open for 14% of the time, Pallas kernels for 15%

profile of v1, /device:TPU:6, one launch (start us, length us, event | category | flops | bytes accessed | tf_op | source)
XLA Modules:
  0.0 447.6 jit_solution(17215288270392794291)
XLA Ops:
  14.7 23.5 %all-gather.5.cloned.1.call-done = bf16[1,1024,1024]{2,1,0:T(8,128)(2,1)} async-done(((bf16[1,256,1024]{2,1,0:T(8,128)(2,1)}), bf16[1,1024,1024]{2,1,0:T(8,128)(2,1)}) %all-gather.5.cloned.1.call-update) | async-done | bytes 2097168 | tf_op jit(solution)/shard_map/all_gather | solution.py:312
  43.3 3.5 fusion.23
  57.9 8.5 %fusion.83 = (f32[2,2,1024]{2,1,0:T(2,128)S(1)}, f32[2,2,1024,1024]{2,3,1,0:T(8,128)}) fusion(bf16[1024,2,2,64]{3,0,2,1:T(8,128)(2,1)S(1)} %bitcast.204, bf16[1024,2,2,64]{3,0,2,1:T(8,128)(2,1)S(1)} %bitcast.202, bf16[1024,2,64]{2,0,1:T(8,128)(2,1)S(1)} %get-tuple-element.88, bf16[1024,2,64]{2,0,1:T(8,128)(2,1)S(1)} %get-tuple-element.87, ...), kind=kOutput, calls=%fused_computation.157 | convolution fusion | flops 1089466368 | bytes 19415040 | tf_op jit(solution)/shard_map/while/body/eval_jaxpr/qhgd,khd->hgqk/dot_general | solution.py:230
  66.5 8.2 %fusion.3 = f32[2,2,1024]{2,1,0:T(2,128)S(1)} fusion(f32[2,2,1024,1024]{2,3,1,0:T(8,128)} %get-tuple-element.105, f32[2,2,1024]{2,1,0:T(2,128)S(1)} %get-tuple-element.104), kind=kLoop, calls=%fused_computation.9 | loop fusion | flops 8384512 | bytes 16809984 | tf_op jit(solution)/shard_map/while/body/eval_jaxpr/reduce_sum | solution.py:242
  75.4 7.8 %fusion.37 = bf16[2,128,2,1024]{3,1,2,0:T(8,128)(2,1)S(1)} fusion(bf16[1024,2,128,1]{0,2,3,1:T(8,128)(2,1)S(1)} %bitcast.220, f32[2,2,1024,1024]{2,3,1,0:T(8,128)} %get-tuple-element.105, f32[2,2,1024]{2,1,0:T(2,128)S(1)} %fusion.3, f32[2,2,1024]{2,1,0:T(2,128)S(1)} %get-tuple-element.104), kind=kOutput, calls=%fused_computation.66 | convolution fusion | flops 1086849024 | bytes 18382848 | tf_op jit(solution)/shard_map/while/body/eval_jaxpr/hgqk,khd->qhgd/dot_general | solution.py:244
  87.0 37.9 %reduce-scatter.5.cloned.1.call-done = bf16[1,256,1024]{2,1,0:T(8,128)(2,1)} async-done(((bf16[1,1024,1024]{2,1,0:T(8,128)(2,1)}), bf16[1,256,1024]{2,1,0:T(8,128)(2,1)}) %reduce-scatter.5.cloned.1.call-update) | async-done | bytes 524304 | tf_op jit(solution)/shard_map/reduce_scatter | solution.py:331
  128.9 25.6 %all-gather.7.cloned.1.call-done = bf16[1,1024,1024]{2,1,0:T(8,128)(2,1)} async-done(((bf16[1,256,1024]{2,1,0:T(8,128)(2,1)}), bf16[1,1024,1024]{2,1,0:T(8,128)(2,1)}) %all-gather.7.cloned.1.call-update) | async-done | bytes 2097168 | tf_op jit(solution)/shard_map/all_gather | solution.py:336
  154.5 5.7 %fusion.19 = f32[1024,768]{1,0:T(8,128)} fusion(bf16[1024,768]{1,0:T(8,128)(2,1)} %param.22, bf16[1,1024,1024]{2,1,0:T(8,128)(2,1)} %all-gather.7.cloned.1.call-done), kind=kOutput, calls=%fused_computation.32 | convolution fusion | flops 1610612736 | bytes 6815744 | tf_op jit(solution)/shard_map/dot_general | solution.py:206
  160.1 3.4 fusion.21
  163.6 18.6 %all-gather.9.cloned.1.call-done = bf16[1,1024,1024]{2,1,0:T(8,128)(2,1)} async-done(((bf16[1,256,1024]{2,1,0:T(8,128)(2,1)}), bf16[1,1024,1024]{2,1,0:T(8,128)(2,1)}) %all-gather.9.cloned.1.call-update) | async-done | bytes 2097168 | tf_op jit(solution)/shard_map/all_gather | solution.py:347
  182.2 7.3 %multiply_convert_fusion = (bf16[1024,768]{1,0:T(8,128)(2,1)S(1)}, bf16[1024,768]{1,0:T(8,128)(2,1)S(1)}, bf16[1024,768]{1,0:T(8,128)(2,1)}) fusion(f32[1024,768]{1,0:T(8,128)} %fusion.21, f32[1024,768]{1,0:T(8,128)} %fusion.19, bf16[768,1024]{1,0:T(8,128)(2,1)S(1)} %copy-done, bf16[1,1024,1024]{2,1,0:T(8,128)(2,1)} %all-gather.9.cloned.1.call-done), kind=kOutput, calls=%fused_computation.19 | convolution fusion | flops 1622409216 | bytes 14680064 | tf_op jit(solution)/shard_map/dot_general | solution.py:216
  192.0 3.2 fusion.12
  195.3 37.9 %reduce-scatter.9.cloned.1.call-done = bf16[1,256,1024]{2,1,0:T(8,128)(2,1)} async-done(((bf16[1,1024,1024]{2,1,0:T(8,128)(2,1)}), bf16[1,256,1024]{2,1,0:T(8,128)(2,1)}) %reduce-scatter.9.cloned.1.call-update) | async-done | bytes 524304 | tf_op jit(solution)/shard_map/reduce_scatter | solution.py:362
  237.6 26.1 %all-gather.11.cloned.1.call-done = bf16[1,1024,1024]{2,1,0:T(8,128)(2,1)} async-done(((bf16[1,256,1024]{2,1,0:T(8,128)(2,1)}), bf16[1,1024,1024]{2,1,0:T(8,128)(2,1)}) %all-gather.11.cloned.1.call-update) | async-done | bytes 2097168 | tf_op jit(solution)/shard_map/all_gather | solution.py:368
  263.8 4.1 fusion.41
  267.9 16.3 %fusion = (f32[2,2,1024]{2,1,0:T(2,128)}, f32[2,1024,1024,2]{2,1,3,0:T(8,128)}) fusion(f32[2,2,1024,1024]{2,3,1,0:T(8,128)} %get-tuple-element.105, f32[2,2,1024]{2,1,0:T(2,128)S(1)} %log_add_fusion, bf16[1024,2,128,1]{0,2,3,1:T(8,128)(2,1)} %bitcast.221, bf16[1024,2,2,128]{0,3,2,1:T(8,128)(2,1)} %bitcast.206), kind=kOutput, calls=%fused_computation.2 | convolution fusion | flops 1086320640 | bytes 35160064 | tf_op jit(solution)/shard_map/while/body/eval_jaxpr/qhgd,khd->hgqk/dot_general | solution.py:259
  284.3 8.6 %fusion.2 = bf16[2,2,1024,1024]{2,3,1,0:T(8,128)(2,1)S(1)} fusion(f32[2,1024,1024,2]{2,1,3,0:T(8,128)} %get-tuple-element.107, f32[2,2,1024,1024]{2,3,1,0:T(8,128)S(1)} %bitcast.192, f32[2,2,1024]{2,1,0:T(2,128)} %get-tuple-element.106, f32[2,2,1024]{2,1,0:T(2,128)S(1)} %log_add_fusion), kind=kLoop, calls=%fused_computation.4 | loop fusion | flops 16777216 | bytes 41975808 | tf_op jit(solution)/shard_map/while/body/eval_jaxpr/convert_element_type | solution.py:269
  292.9 2.8 convolution_multiply_fusion
  295.7 3.4 fusion.50
  299.1 5.1 %fusion.51 = bf16[2,128,1024]{2,1,0:T(8,128)(2,1)} fusion(bf16[1024,2,2,128]{0,3,2,1:T(8,128)(2,1)} %bitcast.207, f32[2,2,1024,1024]{2,3,1,0:T(8,128)S(1)} %bitcast.192, f32[2,2,1024]{2,1,0:T(2,128)S(1)} %log_add_fusion), kind=kOutput, calls=%fused_computation.81 | convolution fusion | flops 1082392576 | bytes 18366464 | tf_op jit(solution)/shard_map/while/body/eval_jaxpr/hgqk,qhgd->khd/dot_general | solution.py:262
  318.7 2.7 fusion.34
  321.5 4.0 copy.121
  325.5 4.0 copy.126
  329.4 5.5 %fusion.38 = bf16[1024,768]{0,1:T(8,128)(2,1)} fusion(bf16[1024,768]{1,0:T(8,128)(2,1)} %get-tuple-element.80, bf16[1,1024,1024]{2,1,0:T(8,128)(2,1)} %all-gather.9.cloned.1.call-done), kind=kOutput, calls=%fused_computation.67 | convolution fusion | flops 1611399168 | bytes 5242880 | tf_op jit(solution)/shard_map/dot_general | solution.py:210
  337.5 4.5 %convert_bitcast_fusion = bf16[1,1024,1024]{2,1,0:T(8,128)(2,1)} fusion(bf16[1024,768]{1,0:T(8,128)(2,1)} %get-tuple-element.80, bf16[768,1024]{1,0:T(8,128)(2,1)S(1)} %copy-done), kind=kOutput, calls=%fused_computation.45 | convolution fusion | flops 1611661312 | bytes 5242880 | tf_op jit(solution)/shard_map/dot_general | solution.py:206
  342.0 4.2 fusion.45
  346.2 4.3 copy.124
  350.5 3.4 fusion.57
  358.4 3.1 fusion.33
  361.5 3.1 fusion.32
  367.6 66.2 %sum_gradients.1 = (f32[32,3840]{1,0:T(8,128)S(1)}, f32[24,128]{1,0:T(8,128)S(1)}) custom-call(bf16[4,4,2,32,3840]{4,3,2,1,0:T(8,128)(2,1)} %constant_dynamic-update-slice_fusion.grads, f32[24,128]{1,0:T(8,128)S(1)} %bitcast.190), custom_call_target="tpu_custom_call" | custom-call | tf_op jit(solution)/shard_map/sum_gradients/pallas_call | solution.py:149
  437.0 3.3 fusion.69
  (236 shorter events, 66.4 us)
Async XLA Ops:
  7.2 175.0 %copy-start = (bf16[768,1024]{1,0:T(8,128)(2,1)S(1)}, bf16[768,1024]{1,0:T(8,128)(2,1)}, u32[]{:S(2)}) copy-start(bf16[768,1024]{1,0:T(8,128)(2,1)} %param.23) | copy-start | bytes 4718596
  7.2 31.0 %all-gather.5.cloned.1.call-start = ((), (), s32[]{:S(2)}) async-start(), calls=%async_computation.4 | async-start | bytes 2621440 | tf_op jit(solution)/shard_map/all_gather | solution.py:312
  10.7 114.2 %reduce-scatter.5.cloned.1.call-start = ((), (), s32[]{:S(2)}) async-start(), calls=%async_computation.5 | async-start | bytes 2621440 | tf_op jit(solution)/shard_map/reduce_scatter | solution.py:331
  11.9 36.1 %copy-start.17 = (f32[1024,64]{0,1:T(8,128)}, f32[1024,64]{0,1:T(8,128)S(1)}, u32[]{:S(2)}) copy-start(f32[1024,64]{0,1:T(8,128)S(1)} %get-tuple-element.102) | copy-start | bytes 786436
  12.1 42.9 %copy-start.11 = (f32[1024,64]{1,0:T(8,128)}, f32[1024,64]{1,0:T(8,128)S(1)}, u32[]{:S(2)}) copy-start(f32[1024,64]{1,0:T(8,128)S(1)} %copy.104) | copy-start | bytes 786436
  43.3 11.3 %copy-start.4 = (f32[1,1024,2,128]{3,1,2,0:T(8,128)}, f32[1,1024,2,128]{3,1,2,0:T(8,128)S(1)}, u32[]{:S(2)}) copy-start(f32[1,1024,2,128]{3,1,2,0:T(8,128)S(1)} %copy.103) | copy-start | bytes 3145732
  56.1 10.3 %copy-start.31 = (bf16[1024,2,64]{2,0,1:T(8,128)(2,1)}, bf16[1024,2,64]{2,0,1:T(8,128)(2,1)S(1)}, u32[]{:S(2)}) copy-start(bf16[1024,2,64]{2,0,1:T(8,128)(2,1)S(1)} %get-tuple-element.87) | copy-start | bytes 786436
  56.1 10.3 %copy-start.33 = (bf16[1024,2,64]{2,0,1:T(8,128)(2,1)}, bf16[1024,2,64]{2,0,1:T(8,128)(2,1)S(1)}, u32[]{:S(2)}) copy-start(bf16[1024,2,64]{2,0,1:T(8,128)(2,1)S(1)} %get-tuple-element.88) | copy-start | bytes 786436
  75.4 8.9 %copy-start.68 = (bf16[512,1024]{1,0:T(8,128)(2,1)S(1)}, bf16[512,1024]{1,0:T(8,128)(2,1)}, u32[]{:S(2)}) copy-start(bf16[512,1024]{1,0:T(8,128)(2,1)} %param.20) | copy-start | bytes 3145732
  86.9 38.0 %copy-start.3 = (bf16[1,256,1024]{2,1,0:T(8,128)(2,1)S(1)}, bf16[1,256,1024]{2,1,0:T(8,128)(2,1)}, u32[]{:S(2)}) copy-start(bf16[1,256,1024]{2,1,0:T(8,128)(2,1)} %param.14) | copy-start | bytes 1572868
  86.9 39.3 %copy-start.48 = (f32[1024]{0:T(1024)S(1)}, f32[1024]{0:T(1024)}, u32[]{:S(2)}) copy-start(f32[1024]{0:T(1024)} %param.25) | copy-start | bytes 12292
  86.9 67.5 %all-gather.7.cloned.1.call-start = ((), (), s32[]{:S(2)}) async-start(), calls=%async_computation.6 | async-start | bytes 2621440 | tf_op jit(solution)/shard_map/all_gather | solution.py:336
  126.2 109.1 %copy-start.51 = (f32[256]{0:T(256)}, f32[256]{0:T(256)S(1)}, u32[]{:S(2)}) copy-start(f32[256]{0:T(256)S(1)} %fusion.77) | copy-start | bytes 3076
  128.3 53.9 %all-gather.9.cloned.1.call-start = ((), (), s32[]{:S(2)}) async-start(), calls=%async_computation.8 | async-start | bytes 2621440 | tf_op jit(solution)/shard_map/all_gather | solution.py:347
  128.8 104.3 %reduce-scatter.9.cloned.1.call-start = ((), (), s32[]{:S(2)}) async-start(), calls=%async_computation.9 | async-start | bytes 2621440 | tf_op jit(solution)/shard_map/reduce_scatter | solution.py:362
  195.2 37.9 %copy-start.6 = (bf16[1,256,1024]{2,1,0:T(8,128)(2,1)S(1)}, bf16[1,256,1024]{2,1,0:T(8,128)(2,1)}, u32[]{:S(2)}) copy-start(bf16[1,256,1024]{2,1,0:T(8,128)(2,1)} %reduce-scatter.5.cloned.1.call-done) | copy-start | bytes 1572868
  195.2 40.1 %copy-start.15 = (bf16[1,256,1024]{2,1,0:T(8,128)(2,1)S(1)}, bf16[1,256,1024]{2,1,0:T(8,128)(2,1)}, u32[]{:S(2)}) copy-start(bf16[1,256,1024]{2,1,0:T(8,128)(2,1)} %param.16) | copy-start | bytes 1572868
  195.2 68.5 %all-gather.11.cloned.1.call-start = ((), (), s32[]{:S(2)}) async-start(), calls=%async_computation.10 | async-start | bytes 2621440 | tf_op jit(solution)/shard_map/all_gather | solution.py:368
  235.3 32.6 %copy-start.58 = (f32[256]{0:T(256)}, f32[256]{0:T(256)S(1)}, u32[]{:S(2)}) copy-start(f32[256]{0:T(256)S(1)} %multiply_multiply_fusion.5) | copy-start | bytes 3076
  237.6 128.4 %reduce-scatter.11.cloned.1.call-start = ((), (), s32[]{:S(2)}) async-start(), calls=%async_computation.11 | async-start | bytes 2621440 | tf_op jit(solution)/shard_map/reduce_scatter | solution.py:395
  267.9 16.3 %slice-start = ((s8[16777216]{0:T(1024)(128)(4,1)}), s8[4194304]{0:T(1024)(128)(4,1)S(1)}, s32[]{:S(2)}) async-start(s8[16777216]{0:T(1024)(128)(4,1)} %bitcast.191), calls=%async_computation.12 | async-start | bytes 8388608
  267.9 16.3 %slice-start.1 = ((s8[16777216]{0:T(1024)(128)(4,1)}), s8[4194304]{0:T(1024)(128)(4,1)S(1)}, s32[]{:S(2)}) async-start(s8[16777216]{0:T(1024)(128)(4,1)} %bitcast.191), calls=%async_computation.13 | async-start | bytes 8388608
  267.9 16.3 %slice-start.2 = ((s8[16777216]{0:T(1024)(128)(4,1)}), s8[4194304]{0:T(1024)(128)(4,1)S(1)}, s32[]{:S(2)}) async-start(s8[16777216]{0:T(1024)(128)(4,1)} %bitcast.191), calls=%async_computation.14 | async-start | bytes 8388608
  267.9 16.3 %slice-start.3 = ((s8[16777216]{0:T(1024)(128)(4,1)}), s8[4194304]{0:T(1024)(128)(4,1)S(1)}, s32[]{:S(2)}) async-start(s8[16777216]{0:T(1024)(128)(4,1)} %bitcast.191), calls=%async_computation.15 | async-start | bytes 8388608
  284.3 8.6 %copy-start.32 = (bf16[1024,2,64]{2,0,1:T(8,128)(2,1)S(1)}, bf16[1024,2,64]{2,0,1:T(8,128)(2,1)}, u32[]{:S(2)}) copy-start(bf16[1024,2,64]{2,0,1:T(8,128)(2,1)} %copy-done.31) | copy-start | bytes 786436
  284.3 8.6 %copy-start.34 = (bf16[1024,2,64]{2,0,1:T(8,128)(2,1)S(1)}, bf16[1024,2,64]{2,0,1:T(8,128)(2,1)}, u32[]{:S(2)}) copy-start(bf16[1024,2,64]{2,0,1:T(8,128)(2,1)} %copy-done.33) | copy-start | bytes 786436
  321.4 115.5 %reduce-scatter.7.cloned.1.call-start = ((), (), s32[]{:S(2)}) async-start(), calls=%async_computation.7 | async-start | bytes 2621440 | tf_op jit(solution)/shard_map/reduce_scatter | solution.py:343
  367.5 66.3 %copy-start.57 = (f32[256]{0:T(256)S(1)}, f32[256]{0:T(256)}, u32[]{:S(2)}) copy-start(f32[256]{0:T(256)} %copy-done.56) | copy-start | bytes 3076
  367.6 69.4 %copy-start.16 = (bf16[1,256,1024]{2,1,0:T(8,128)(2,1)S(1)}, bf16[1,256,1024]{2,1,0:T(8,128)(2,1)}, u32[]{:S(2)}) copy-start(bf16[1,256,1024]{2,1,0:T(8,128)(2,1)} %param.16) | copy-start | bytes 1572868
  367.6 69.4 %copy-start.49 = (f32[1024]{0:T(1024)S(1)}, f32[1024]{0:T(1024)}, u32[]{:S(2)}) copy-start(f32[1024]{0:T(1024)} %param.25) | copy-start | bytes 12292
  367.6 69.4 %copy-start.52 = (f32[256]{0:T(256)S(1)}, f32[256]{0:T(256)}, u32[]{:S(2)}) copy-start(f32[256]{0:T(256)} %copy-done.51) | copy-start | bytes 3076
  367.6 69.4 %copy-start.59 = (f32[256]{0:T(256)S(1)}, f32[256]{0:T(256)}, u32[]{:S(2)}) copy-start(f32[256]{0:T(256)} %copy-done.58) | copy-start | bytes 3076
  (55 other events, 147.7 us)
Sparse Core Ops, SparseCore 0:
  10.8 27.3 all-gather.4
  87.1 37.7 reduce-scatter.4
  128.4 26.0 all-gather.6
  156.1 26.0 all-gather.8
  195.4 37.7 reduce-scatter.8
  237.7 26.0 all-gather.10
  321.6 37.7 reduce-scatter.10
  362.2 37.7 reduce-scatter.6

commit v2 on v0

v2 whole, which is shorter than its diff:
```python
import math

import jax
import jax.numpy as jnp
import numpy as np
from jax import lax
from jax.experimental import pallas as pl
from jax.experimental.pallas import tpu as pltpu
from jax.sharding import PartitionSpec as P

MESH = pl.DeviceIdType.MESH
BF16 = jnp.bfloat16
F32 = jnp.float32
EPSILON = 1e-06
ROPE_BASE = 1000000.0
BLOCK = 256
HEAD = 128
QUERY_SCALE = math.log2(math.e) / math.sqrt(HEAD)
PARTNERS = ("core", "far", "y1", "y2", "z1", "z2", "x")
ORDERS = (("y1", "y2", "z1", "z2"), ("y2", "y1", "z2", "z1"), ("z1", "z2", "y1", "y2"), ("z2", "z1", "y2", "y1"))
MLP_WIDTHS = (640, 640, 512, 512)
ATTN_WIDTHS = (384, 384, 384, 384)
GAIN_ORDER = ("core", "y1", "y2", "z1", "z2", "x", "far")

SCRATCH = (
    ("w_qkv", (1024, 1024), BF16),
    ("t_qkv", (1024, 1024), BF16),
    ("w_down", (768, 1024), BF16),
    ("t_gu", (1536, 1024), BF16),
    ("mlp_mix", (4, 4, 64, 2304), BF16),
    ("attn_mix", (4, 4, 64, 1536), BF16),
    ("h1", (1024, 1024), BF16),
    ("h2", (1024, 1024), BF16),
    ("da", (1024, 1024), BF16),
    ("norm_qk", (768, 1024), BF16),
    ("root_qk", (8, 1024), F32),
    ("ob", (512, 1024), BF16),
    ("qs", (2, 4, 128, 512), BF16),
    ("ks_t", (256, 1024), BF16),
    ("ks", (2, 1024, 128), BF16),
    ("v_t", (2, 144, 1024), BF16),
    ("v", (2, 1024, 128), BF16),
    ("p", (20, 4, 64, 512), BF16),
    ("inv", (2, 4, 8, 512), F32),
    ("inner", (2, 4, 8, 512), F32),
    ("mask", (10, 256, 256), BF16),
    ("hidden", (768, 1024), BF16),
    ("dgu", (1536, 1024), BF16),
    ("cosine", (64, 1024), F32),
    ("sine", (64, 1024), F32),
    ("x_t", (1024, 256), BF16),
    ("resid", (1024, 256), F32),
    ("gain1", (1024, 128), F32),
    ("gain2", (1024, 128), F32),
    ("gain_q", (128, 128), F32),
    ("gain_k", (128, 128), F32),
    ("gain_sum", (1024, 128), F32),
    ("gain_q_sum", (128, 256), F32),
    ("gain_k_sum", (128, 256), F32),
    ("root1", (8, 256), F32),
    ("root2", (8, 256), F32),
    ("acc_o", (144, 512), F32),
    ("acc_q", (128, 512), F32),
    ("keep_far", (1024, 256), F32),
    ("keep_own", (1024, 256), F32),
    ("sib_out", (2, 1024, 256), BF16),
    ("sib_in", (2, 1024, 256), BF16),
    ("far_out", (1024, 256), BF16),
    ("far_in", (1024, 256), BF16),
    ("mlp_own", (1024, 256), F32),
    ("mlp_sib_out", (2, 1024, 256), BF16),
    ("mlp_sib_in", (2, 1024, 256), BF16),
    ("mlp_far_out", (1024, 256), BF16),
    ("mlp_far_in", (1024, 256), BF16),
    ("mlp_halves", (16, 4, 64, 640), BF16),
    ("sums", (32, 3840), F32),
    ("gain_parts", (14, 8, 1024), F32),
)
SEMAPHORES = 120


class Box:
    pass


class Place:
    def __init__(self):
        dp = lax.axis_index("dp")
        tensor = lax.axis_index("tensor")
        self.z, self.y, self.x = dp // 8, (dp // 2) % 4, dp % 2
        self.far, self.core = tensor // 2, tensor % 2
        self.me = tensor
        self.sib = self.far * 2 + 1 - self.core
        self.across = (1 - self.far) * 2 + self.core
        self.across_sib = (1 - self.far) * 2 + 1 - self.core

    def near(self, name):
        return step_of(name, self.y if name[0] == "y" else self.z)

    def device(self, name):
        z, y, x, far, core = self.z, self.y, self.x, self.far, self.core
        if name[0] == "y":
            y = self.near(name)
        elif name[0] == "z":
            z = self.near(name)
        elif name == "x":
            x = 1 - x
        elif name == "far":
            far = 1 - far
        else:
            core = 1 - core
        return ((z * 4 + y) * 2 + x, far * 2 + core)


def step_of(name, value):
    return value + 1 - 2 * (value % 2) if name[1] == "1" else 3 - value


def nn(left, right):
    return lax.dot_general(left, right, (((1,), (0,)), ((), ())), preferred_element_type=F32)


def nt(left, right):
    return lax.dot_general(left, right, (((1,), (1,)), ((), ())), preferred_element_type=F32)


def span(index, size=BLOCK):
    return pl.ds(pl.multiple_of(index * size, size), size)


def loop(count, body):
    def step(index, carry):
        body(index)
        return carry

    lax.fori_loop(0, count, step, 0)


def twice(values):
    return jnp.concatenate([values, values], axis=1)


def fold(values):
    return jnp.sum(values.reshape(values.shape[0] // 8, 8, values.shape[1]), axis=0)


class Links:
    def __init__(self, place, sems):
        self.place, self.sems, self.used, self.sent = place, sems, 0, []

    def send(self, src, dst, name):
        copy = pltpu.make_async_remote_copy(
            src_ref=src,
            dst_ref=dst,
            send_sem=self.sems.at[0, self.used],
            recv_sem=self.sems.at[1, self.used],
            device_id=self.place.device(name),
            device_id_type=MESH,
        )
        self.used += 1
        copy.start()
        return copy


class Gather:
    def __init__(self, links, at):
        self.links, self.at = links, at
        self.far, self.sib, self.passed = [], [], []

    def send(self, half):
        block = self.at(half, self.links.place.me)
        self.far.append(self.links.send(block, block, "far"))
        self.sib.append(self.links.send(block, block, "core"))

    def pass_on(self):
        for half, copy in enumerate(self.far):
            copy.wait_recv()
            block = self.at(half, self.links.place.across)
            self.passed.append(self.links.send(block, block, "core"))

    def near_ready(self):
        for copy in self.sib:
            copy.wait_recv()

    def far_ready(self):
        for copy in self.passed:
            copy.wait_recv()

    def drain(self):
        for copy in self.far + self.sib + self.passed:
            copy.wait_send()


class Reduce:
    def __init__(self, links, sib_out, sib_in, far_out, far_in):
        self.links = links
        self.sib_out, self.sib_in, self.far_out, self.far_in = sib_out, sib_in, far_out, far_in
        self.copies = [None, None]
        self.far = []

    def to_sibling(self, index):
        self.copies[index] = self.links.send(self.sib_out.at[index], self.sib_in.at[index], "core")

    def make_far(self, keep, half):
        if half == 0:
            self.copies[0].wait_recv()

        def body(i):
            rows = span(i + 4 * half, 128)
            self.far_out[rows, :] = (keep[rows, :] + self.sib_in[0, rows, :].astype(F32)).astype(BF16)

        loop(4, body)

    def send_far(self, half):
        rows = pl.ds(512 * half, 512)
        self.far.append(self.links.send(self.far_out.at[rows], self.far_in.at[rows], "far"))

    def arrive(self):
        self.copies[1].wait_recv()
        for copy in self.far:
            copy.wait_recv()

    def total(self, keep, rows):
        return keep[rows, :] + self.sib_in[1, rows, :].astype(F32) + self.far_in[rows, :].astype(F32)

    def drain(self):
        for copy in self.copies + self.far:
            copy.wait_send()


class DpSum:
    def __init__(self, links, source, widths, bufs, out, out_first):
        self.links, self.source, self.bufs, self.out, self.out_first = links, source, bufs, out, out_first
        self.widths = widths
        self.first = [sum(widths[:k]) for k in range(4)]
        self.phase = -1
        self.flying = [[], [], [], []]
        self.sent = []

    def held(self, stream, phase):
        w = self.widths[stream]
        at = 4 * stream
        if phase == 0:
            return self.bufs.at[pl.ds(at, 2), :, :, pl.ds(0, w)]
        if phase == 1:
            return self.bufs.at[at + 2, :, :, pl.ds(0, w)]
        if phase == 2:
            return self.bufs.at[at + 3, pl.ds(0, 2), :, pl.ds(0, w)]
        if phase == 3:
            return self.bufs.at[at + 3, 2, :, pl.ds(0, w)]
        return self.bufs.at[at + 3, 3, pl.ds(0, 32), pl.ds(0, w)]

    def begin(self, stream, phase):
        place, send = self.links.place, self.links.send
        order = ORDERS[stream]
        into = self.held(stream, phase)
        if phase == 4:
            theirs = self.held(stream, 3).at[span(1 - place.x, 32)]
            return [send(theirs, into, "x")]
        name = order[phase]
        if phase in (1, 3):
            return [send(self.held(stream, phase - 1).at[1], into, name)]
        there = place.near(name)
        copies = []
        for j, at in enumerate((there, step_of(order[phase + 1], there))):
            if phase == 2:
                source = self.held(stream, 1).at[at]
            else:
                columns = pl.ds(self.first[stream], self.widths[stream])
                source = self.source.at[:, at, :, columns] if name[0] == "y" else self.source.at[at, :, :, columns]
            copies.append(send(source, into.at[j], name))
        return copies

    def finish(self, stream, phase):
        place = self.links.place
        order, first, w = ORDERS[stream], self.first[stream], self.widths[stream]
        at = 4 * stream
        bufs = self.bufs
        for copy in self.flying[stream]:
            copy.wait_recv()
        if phase == 4:
            mine = bufs[at + 3, 2, span(place.x, 32), pl.ds(0, w)].astype(F32)
            columns = pl.ds(self.out_first + first, w)
            self.out[:, columns] = bufs[at + 3, 3, pl.ds(0, 32), pl.ds(0, w)].astype(F32) + mine
        elif phase == 3:
            bufs[at + 3, 2, :, pl.ds(0, w)] += bufs[at + 3, 0, :, pl.ds(0, w)]
        elif phase == 1:
            for k in range(4):
                bufs[at + 2, k, :, pl.ds(0, w)] += bufs[at, k, :, pl.ds(0, w)]
        else:
            name = order[phase]
            mine = place.y if name[0] == "y" else place.z
            for j, own in enumerate((mine, step_of(order[phase + 1], mine))):
                if phase == 2:
                    bufs[at + 3, j, :, pl.ds(0, w)] += bufs[at + 2, own, :, pl.ds(0, w)]
                    continue
                for k in range(4):
                    lead = (k, own) if name[0] == "y" else (own, k)
                    bufs[at + j, k, :, pl.ds(0, w)] += self.source[(*lead, slice(None), pl.ds(first, w))]

    def advance(self):
        for stream in range(4):
            if self.phase >= 0:
                self.finish(stream, self.phase)
                self.sent += self.flying[stream]
            if self.phase < 4:
                self.flying[stream] = self.begin(stream, self.phase + 1)
        self.phase += 1

    def drain(self):
        for copy in self.sent:
            copy.wait_send()


def head_forward(raw, gain, cosine, sine):
    root = lax.rsqrt(jnp.mean(raw * raw, axis=0, keepdims=True) + EPSILON)
    normed = raw * root
    scaled = normed * gain
    first, second = scaled[:64], scaled[64:]
    turned = jnp.concatenate([first * cosine - second * sine, second * cosine + first * sine], axis=0)
    return normed, root, turned


def head_backward(grad, normed, root, gain, cosine, sine):
    first, second = grad[:64], grad[64:]
    turned = jnp.concatenate([first * cosine + second * sine, second * cosine - first * sine], axis=0)
    scaled = turned * gain
    inner = jnp.mean(scaled * normed, axis=0, keepdims=True)
    return root * (scaled - normed * inner), turned * normed


def layer_kernel(
    x, starts, dy, wq, wk, wv, wo, wg, wu, wd, g1, g2, gq, gk, frequency,
    out, grad_x, out_q, out_k, out_v, out_o, out_g, out_u, out_d, out_g1, out_g2, out_gq, out_gk,
    *scratch,
):
    s = Box()
    for (name, _, _), ref in zip(SCRATCH, scratch):
        setattr(s, name, ref)
    link_sems, load_sems, ready = scratch[len(SCRATCH) :]
    place = Place()
    links = Links(place, link_sems)
    me, sib, across, across_sib = place.me, place.sib, place.across, place.across_sib

    barrier = pltpu.get_barrier_semaphore()
    for name in PARTNERS:
        pl.semaphore_signal(barrier, inc=1, device_id=place.device(name), device_id_type=MESH)
    pl.semaphore_wait(barrier, len(PARTNERS))

    loads = []

    def load(src, dst):
        copy = pltpu.make_async_copy(src, dst, load_sems.at[len(loads)])
        copy.start()
        loads.append(copy)

    load(wq, s.w_qkv.at[:, pl.ds(0, 512)])
    load(wk, s.w_qkv.at[:, pl.ds(512, 256)])
    load(wv, s.w_qkv.at[:, pl.ds(768, 256)])
    load(wo, s.h2.at[pl.ds(0, 512)])
    load(wg, s.mlp_mix.at[:, :, :, pl.ds(0, 768)])
    load(wu, s.mlp_mix.at[:, :, :, pl.ds(768, 768)])
    load(wd, s.w_down)

    def first_norm(i):
        rows = span(i, 64)
        xs = x[rows, :].astype(F32)
        root = lax.rsqrt(jnp.mean(xs * xs, axis=1, keepdims=True) + EPSILON)
        out[rows, :] = (xs * root * g1[...]).astype(BF16)

    loop(4, first_norm)
    gather_h1 = Gather(links, lambda half, b: s.h1.at[pl.ds(512 * half, 512), span(b)])
    for half in range(2):
        for j in range(2):
            s.h1[pl.ds(512 * half + 256 * j, 256), span(me)] = out[:, pl.ds(512 * half + 256 * j, 256)].T
        gather_h1.send(half)

    def dy_in(i):
        s.attn_mix[i, :, :, span(me)] = dy[:, span(i)].T.reshape(4, 64, BLOCK)

    loop(4, dy_in)
    for k in range(3):
        loads[k].wait()

    def turn_qkv(i):
        s.t_qkv[span(i), :] = s.w_qkv[:, span(i)].T

    loop(4, turn_qkv)

    place_row = lax.broadcasted_iota(jnp.int32, (8, 1024), 1)
    start_row = jnp.zeros((8, 1024), jnp.int32)
    for d in range(4):
        start_row = jnp.maximum(start_row, jnp.where(place_row >= starts[0, d], starts[0, d], 0))
    position = (place_row - start_row).astype(F32)
    for i in range(8):
        lanes = pl.ds(128 * i, 128)
        angle = frequency[...] * position[0:1, 128 * i : 128 * i + 128]
        s.cosine[:, lanes] = jnp.cos(angle)
        s.sine[:, lanes] = jnp.sin(angle)
    for qb in range(4):
        first = start_row[0:1, qb * 256 : qb * 256 + 256]
        query = lax.broadcasted_iota(jnp.int32, (256, 256), 1) + qb * 256
        for kb in range(qb + 1):
            key = lax.broadcasted_iota(jnp.int32, (256, 256), 0) + kb * 256
            allowed = (key <= query) & (key >= first)
            s.mask[qb * (qb + 1) // 2 + kb] = jnp.where(allowed, 1.0, 0.0).astype(BF16)

    s.gain1[...] = jnp.broadcast_to(g1[...], (128, 1024)).T
    s.gain2[...] = jnp.broadcast_to(g2[...], (128, 1024)).T
    s.gain_q[...] = jnp.broadcast_to(gq[...], (128, 128)).T
    s.gain_k[...] = jnp.broadcast_to(gk[...], (128, 128)).T
    s.gain_q_sum[...] = jnp.zeros((128, 256), F32)
    s.gain_k_sum[...] = jnp.zeros((128, 256), F32)
    for g in range(2):
        s.v_t[g, pl.ds(128, 16), :] = jnp.ones((16, 1024), BF16)

    def x_in(i, total):
        turned = x[:, span(i)].astype(F32).T
        s.x_t[span(i), :] = turned.astype(BF16)
        return total + fold(turned * turned)

    square = lax.fori_loop(0, 4, x_in, jnp.zeros((8, BLOCK), F32))
    root = lax.rsqrt(jnp.sum(square, axis=0, keepdims=True) / 1024.0 + EPSILON)
    s.root1[...] = jnp.broadcast_to(root, (8, BLOCK))

    loads[3].wait()

    def turn_out(i):
        s.attn_mix[i, :, :, pl.ds(1024, 512)] = s.h2[pl.ds(0, 512), span(i)].T.reshape(4, 64, 512)

    loop(4, turn_out)
    loads[4].wait()
    loads[5].wait()

    def turn_gu(i):
        for z in range(4):
            s.t_gu[span(i), pl.ds(256 * z, 256)] = s.mlp_mix[z, :, :, span(i)].reshape(256, 256).T

    loop(6, turn_gu)
    loads[6].wait()

    def turn_down(i):
        s.mlp_mix[i, :, :, pl.ds(1536, 768)] = s.w_down[:, span(i)].T.reshape(4, 64, 768)

    loop(4, turn_down)

    def project(b):
        columns = span(b)
        cosine, sine = s.cosine[:, columns], s.sine[:, columns]
        for g in range(2):
            raw = nn(s.t_qkv[pl.ds(256 * g, 256), :], s.h1[:, columns])
            gain = twice(s.gain_q[...] * QUERY_SCALE)
            for k in range(2):
                head = 2 * g + k
                normed, root, turned = head_forward(raw[128 * k : 128 * k + 128], gain, cosine, sine)
                s.norm_qk[pl.ds(128 * head, 128), columns] = normed.astype(BF16)
                s.root_qk[pl.ds(head, 1), columns] = root
                s.qs[g, b, :, pl.ds(256 * k, 256)] = turned.astype(BF16)
        raw = nn(s.t_qkv[pl.ds(512, 256), :], s.h1[:, columns])
        gain = twice(s.gain_k[...])
        for g in range(2):
            normed, root, turned = head_forward(raw[128 * g : 128 * g + 128], gain, cosine, sine)
            s.norm_qk[pl.ds(512 + 128 * g, 128), columns] = normed.astype(BF16)
            s.root_qk[pl.ds(4 + g, 1), columns] = root
            s.ks_t[pl.ds(128 * g, 128), columns] = turned.astype(BF16)
            s.ks[g, columns, :] = turned.astype(BF16).T
        raw = nn(s.t_qkv[pl.ds(768, 256), :], s.h1[:, columns]).astype(BF16)
        for g in range(2):
            s.v_t[g, pl.ds(0, 128), columns] = raw[128 * g : 128 * g + 128]
            s.v[g, columns, :] = raw[128 * g : 128 * g + 128].T

    gather_h1.near_ready()
    loop(2, lambda i: project(place.far * 2 + i))
    gather_h1.pass_on()
    gather_dy = Gather(links, lambda half, b: s.attn_mix.at[pl.ds(2 * half, 2), :, :, span(b)])
    gather_dy.send(0)
    gather_dy.send(1)
    gather_h1.far_ready()
    loop(2, lambda i: project((1 - place.far) * 2 + i))

    def attend(qb):
        def group(g):
            s.acc_o[...] = jnp.zeros((144, 512), F32)

            def keys(kb):
                at = qb * (qb + 1) // 2 + kb
                scores = nn(s.ks[g, span(kb), :], s.qs[g, qb])
                weights = jnp.exp2(scores).astype(BF16) * twice(s.mask[at])
                s.p[g * 10 + at] = weights.reshape(4, 64, 512)
                s.acc_o[...] += nn(s.v_t[g, :, span(kb)], weights)

            loop(qb + 1, keys)
            inverse = 1.0 / s.acc_o[pl.ds(128, 8), :]
            s.inv[g, qb] = inverse
            attended = (s.acc_o[pl.ds(0, 128), :] * inverse[0:1]).astype(BF16)
            rows = pl.multiple_of(g * 256, 256)
            s.ob[pl.ds(rows, 128), span(qb)] = attended[:, :256]
            s.ob[pl.ds(rows + 128, 128), span(qb)] = attended[:, 256:]

        loop(2, group)

    def out_product(b, store):
        def body(i):
            store(i, nn(s.attn_mix[i, :, :, pl.ds(1024, 512)].reshape(256, 512), s.ob[:, span(b)]))

        loop(4, body)

    def to(ref, index=None):
        def store(i, values):
            if index is None:
                ref[span(i), :] = values.astype(ref.dtype)
            else:
                ref[index, span(i), :] = values.astype(ref.dtype)

        return store

    sum_attn = Reduce(links, s.sib_out, s.sib_in, s.far_out, s.far_in)
    attend(across_sib)
    out_product(across_sib, to(s.sib_out, 0))
    sum_attn.to_sibling(0)
    attend(across)
    out_product(across, to(s.keep_far))
    for half in range(2):
        sum_attn.make_far(s.keep_far, half)
        sum_attn.send_far(half)
    attend(sib)
    out_product(sib, to(s.sib_out, 1))
    sum_attn.to_sibling(1)
    attend(me)
    out_product(me, to(s.keep_own))
    gather_dy.near_ready()
    gather_dy.pass_on()
    sum_attn.arrive()

    def second_norm(i, total):
        rows = span(i, 128)
        x1 = s.x_t[rows, :].astype(F32) + sum_attn.total(s.keep_own, rows)
        s.resid[rows, :] = x1
        return total + fold(x1 * x1)

    square = lax.fori_loop(0, 8, second_norm, jnp.zeros((8, BLOCK), F32))
    root2 = lax.rsqrt(jnp.sum(square, axis=0, keepdims=True) / 1024.0 + EPSILON)
    s.root2[...] = jnp.broadcast_to(root2, (8, BLOCK))
    gather_h2 = Gather(links, lambda half, b: s.h2.at[pl.ds(512 * half, 512), span(b)])
    for half in range(2):

        def scale_rows(i, half=half):
            rows = span(i + 4 * half, 128)
            s.h2[rows, span(me)] = (s.resid[rows, :] * s.root2[0:1] * twice(s.gain2[rows, :])).astype(BF16)

        loop(4, scale_rows)
        gather_h2.send(half)
    sum_attn.drain()
    gather_dy.far_ready()

    def dy_rows(i):
        return s.attn_mix[i, :, :, pl.ds(0, 1024)].reshape(256, 1024)

    def feed(b):
        columns = span(b)

        def body(j):
            normed = s.h2[:, columns]
            gate = nn(s.t_gu[span(j), :], normed)
            up = nn(s.t_gu[pl.ds(pl.multiple_of(768 + 256 * j, 256), 256), :], normed)
            grad = nn(s.w_down[span(j), :], s.attn_mix[:, :, :, columns].reshape(1024, 256))
            open_gate = jax.nn.sigmoid(gate)
            silu = gate * open_gate
            s.hidden[span(j), columns] = (silu * up).astype(BF16)
            s.dgu[span(j), columns] = (grad * up * open_gate * (1.0 + gate * (1.0 - open_gate))).astype(BF16)
            s.dgu[pl.ds(pl.multiple_of(768 + 256 * j, 256), 256), columns] = (grad * silu).astype(BF16)

        loop(3, body)

    def feed_back(b, store):
        def body(i):
            store(i, nn(s.mlp_mix[i, :, :, pl.ds(0, 1536)].reshape(256, 1536), s.dgu[:, span(b)]))

        loop(4, body)

    def mlp_product(b, store):
        def body(i):
            store(i, nn(s.mlp_mix[i, :, :, pl.ds(1536, 768)].reshape(256, 768), s.hidden[:, span(b)]))

        loop(4, body)

    sum_dh2 = Reduce(links, s.sib_out, s.sib_in, s.far_out, s.far_in)
    gather_h2.near_ready()
    feed(sib)
    feed_back(sib, to(s.sib_out, 1))
    sum_dh2.to_sibling(1)
    feed(me)
    feed_back(me, to(s.keep_own))
    gather_h2.pass_on()
    gather_h2.far_ready()
    feed(across_sib)
    feed_back(across_sib, to(s.sib_out, 0))
    sum_dh2.to_sibling(0)
    feed(across)
    feed_back(across, to(s.keep_far))
    for half in range(2):
        sum_dh2.make_far(s.keep_far, half)
        sum_dh2.send_far(half)

    sum_mlp = Reduce(links, s.mlp_sib_out, s.mlp_sib_in, s.mlp_far_out, s.mlp_far_in)
    mlp_product(across_sib, to(s.mlp_sib_out, 0))
    sum_mlp.to_sibling(0)
    mlp_product(sib, to(s.mlp_sib_out, 1))
    sum_mlp.to_sibling(1)
    mlp_product(across, to(s.keep_far))

    def mlp_mine(i, values):
        s.mlp_own[span(i), :] = s.resid[span(i), :] + values

    mlp_product(me, mlp_mine)
    for half in range(2):
        sum_mlp.make_far(s.keep_far, half)

    def down_grad(i):
        s.mlp_mix[i, :, :, pl.ds(1536, 768)] = nt(dy_rows(i), s.hidden[...]).astype(BF16).reshape(4, 64, 768)

    loop(4, down_grad)

    def gate_up_grad(i):
        for j in range(3):
            values = nt(s.h2[span(i), :], s.dgu[pl.ds(512 * j, 512), :]).astype(BF16)
            s.mlp_mix[i, :, :, pl.ds(512 * j, 512)] = values.reshape(4, 64, 512)

    loop(4, gate_up_grad)
    gather_h2.drain()
    again = pltpu.make_async_copy(wo, s.h2.at[pl.ds(0, 512)], load_sems.at[7])
    again.start()
    dp_mlp = DpSum(links, s.mlp_mix, MLP_WIDTHS, s.mlp_halves, s.sums, 1536)
    dp_mlp.advance()

    sum_dh2.arrive()

    def norm_back_sum(i, total):
        rows = span(i, 128)
        grad = sum_dh2.total(s.keep_own, rows)
        s.keep_own[rows, :] = grad
        product = grad * (s.resid[rows, :] * s.root2[0:1])
        s.gain_sum[rows, :] = product[:, :128] + product[:, 128:]
        return total + fold(product * twice(s.gain2[rows, :]))

    inner = lax.fori_loop(0, 8, norm_back_sum, jnp.zeros((8, BLOCK), F32))
    inner = jnp.sum(inner, axis=0, keepdims=True) / 1024.0
    gather_da = Gather(links, lambda half, b: s.da.at[pl.ds(512 * half, 512), span(b)])
    for half in range(2):

        def norm_back(i, half=half):
            rows = span(i + 4 * half, 128)
            scaled = s.keep_own[rows, :] * twice(s.gain2[rows, :])
            normed = s.resid[rows, :] * s.root2[0:1]
            own = s.attn_mix[2 * half + i // 2, pl.ds(2 * (i % 2), 2), :, span(me)].reshape(128, BLOCK).astype(F32)
            dx1 = own + s.root2[0:1] * (scaled - normed * inner)
            s.resid[rows, :] = dx1
            s.da[rows, span(me)] = dx1.astype(BF16)

        loop(4, norm_back)
        gather_da.send(half)
    sum_dh2.drain()
    s.gain_parts[0, 1:2, :] = jnp.sum(s.gain_sum[...].T, axis=0, keepdims=True)
    dp_mlp.advance()

    s.keep_own[...] = jnp.zeros((1024, 256), F32)
    s.keep_far[...] = jnp.zeros((1024, 256), F32)
    again.wait()

    def out_back(b):
        def body(g):
            grads = nn(s.h2[span(g), :], s.da[:, span(b)])
            both = jnp.concatenate([grads[:128], grads[128:]], axis=1) * s.inv[g, b][0:1]
            rows = pl.multiple_of(g * 256, 256)
            outs = jnp.concatenate([s.ob[pl.ds(rows, 128), span(b)], s.ob[pl.ds(rows + 128, 128), span(b)]], axis=1)
            s.inner[g, b] = jnp.broadcast_to(jnp.sum(both * outs.astype(F32), axis=0, keepdims=True), (8, 512))
            s.t_gu[span(g * 4 + b, 128), pl.ds(0, 512)] = both.astype(BF16)

        loop(2, body)

    gather_da.near_ready()
    loop(2, lambda i: out_back(place.far * 2 + i))
    gather_da.pass_on()
    for half in range(2):
        sum_mlp.send_far(half)
    gather_da.far_ready()
    loop(2, lambda i: out_back((1 - place.far) * 2 + i))

    def out_grad(i):
        s.attn_mix[i, :, :, pl.ds(1024, 512)] = nt(s.da[span(i), :], s.ob[...]).astype(BF16).reshape(4, 64, 512)

    loop(4, out_grad)
    dp_mlp.advance()

    def attend_back(qb):
        columns = span(qb)
        cosine, sine = s.cosine[:, columns], s.sine[:, columns]
        gain = twice(s.gain_q[...])
        for g in range(2):
            s.acc_q[...] = jnp.zeros((128, 512), F32)

            def keys(kb, g=g):
                at = g * 10 + qb * (qb + 1) // 2 + kb
                rows = span(kb)
                grads = s.t_gu[span(g * 4 + qb, 128), pl.ds(0, 512)]
                weights = s.p[at].reshape(256, 512)
                slope = nn(s.v[g, rows, :], grads) - s.inner[g, qb][0:1]
                ds = (weights.astype(F32) * slope).astype(BF16)
                s.keep_own[rows, pl.ds(128 * g, 128)] += nt(weights, grads)
                s.keep_far[rows, pl.ds(128 * g, 128)] += nt(ds, s.qs[g, qb])
                s.acc_q[...] += nn(s.ks_t[pl.ds(128 * g, 128), rows], ds)

            loop(qb + 1, keys)
            for k in range(2):
                head = 2 * g + k
                grad, gain_part = head_backward(
                    s.acc_q[:, pl.ds(256 * k, 256)] * (1.0 / math.sqrt(HEAD)),
                    s.norm_qk[pl.ds(128 * head, 128), columns].astype(F32),
                    s.root_qk[pl.ds(head, 1), columns],
                    gain,
                    cosine,
                    sine,
                )
                s.t_qkv[pl.ds(128 * head, 128), columns] = grad.astype(BF16)
                s.gain_q_sum[...] += gain_part

    loop(2, attend_back)
    dp_mlp.advance()
    loop(2, lambda i: attend_back(2 + i))
    dp_mlp.advance()

    for k, name in enumerate(PARTNERS[2:]):
        pl.semaphore_signal(ready.at[k], inc=1, device_id=place.device(name), device_id_type=MESH)

    def key_back(b):
        columns = span(b)
        cosine, sine = s.cosine[:, columns], s.sine[:, columns]
        gain = twice(s.gain_k[...])
        for g in range(2):
            grad, gain_part = head_backward(
                s.keep_far[columns, pl.ds(128 * g, 128)].T * math.log(2.0),
                s.norm_qk[pl.ds(512 + 128 * g, 128), columns].astype(F32),
                s.root_qk[pl.ds(4 + g, 1), columns],
                gain,
                cosine,
                sine,
            )
            s.t_qkv[pl.ds(512 + 128 * g, 128), columns] = grad.astype(BF16)
            s.gain_k_sum[...] += gain_part
            s.t_qkv[pl.ds(768 + 128 * g, 128), columns] = s.keep_own[columns, pl.ds(128 * g, 128)].T.astype(BF16)

    loop(4, key_back)

    def in_back(b, store):
        def body(i):
            store(i, nn(s.w_qkv[span(i), :], s.t_qkv[:, span(b)]))

        loop(4, body)

    sum_dh1 = Reduce(links, s.sib_out, s.sib_in, s.far_out, s.far_in)
    in_back(across_sib, to(s.sib_out, 0))
    sum_dh1.to_sibling(0)
    in_back(across, to(s.keep_far))
    for half in range(2):
        sum_dh1.make_far(s.keep_far, half)
        sum_dh1.send_far(half)
    gather_dy.drain()

    def qkv_grad(i):
        for j in range(2):
            values = nt(s.h1[span(i), :], s.t_qkv[pl.ds(512 * j, 512), :]).astype(BF16)
            s.attn_mix[i, :, :, pl.ds(512 * j, 512)] = values.reshape(4, 64, 512)

    loop(4, qkv_grad)
    for k in range(5):
        pl.semaphore_wait(ready.at[k], 1)
    dp_mlp.advance()
    dp_attn = DpSum(links, s.attn_mix, ATTN_WIDTHS, s.p, s.sums, 0)
    dp_attn.advance()
    in_back(sib, to(s.sib_out, 1))
    sum_dh1.to_sibling(1)
    in_back(me, to(s.keep_own))
    for row, part in ((0, s.gain_q_sum), (1, s.gain_k_sum)):
        both = part[:, pl.ds(0, 128)] + part[:, pl.ds(128, 128)]
        s.gain_parts[0, 2:3, pl.ds(128 * row, 128)] = jnp.sum(both.T, axis=0, keepdims=True)
    s.gain_parts[0, 2:3, pl.ds(256, 768)] = jnp.zeros((1, 768), F32)
    s.gain_parts[0, pl.ds(3, 5), :] = jnp.zeros((5, 1024), F32)

    sum_mlp.arrive()

    def layer_out(i):
        out[:, span(i)] = sum_mlp.total(s.mlp_own, span(i)).T.astype(BF16)

    loop(4, layer_out)
    dp_attn.advance()

    sum_dh1.arrive()

    def last_back_sum(i, total):
        rows = span(i, 128)
        grad = sum_dh1.total(s.keep_own, rows)
        s.keep_own[rows, :] = grad
        product = grad * (s.x_t[rows, :].astype(F32) * s.root1[0:1])
        s.gain_sum[rows, :] = product[:, :128] + product[:, 128:]
        return total + fold(product * twice(s.gain1[rows, :]))

    inner = lax.fori_loop(0, 8, last_back_sum, jnp.zeros((8, BLOCK), F32))
    inner = jnp.sum(inner, axis=0, keepdims=True) / 1024.0
    s.gain_parts[0, 0:1, :] = jnp.sum(s.gain_sum[...].T, axis=0, keepdims=True)
    gain_copies = [links.send(s.gain_parts.at[0], s.gain_parts.at[7], GAIN_ORDER[0])]

    def last_back(i):
        rows = span(i)
        scaled = s.keep_own[rows, :] * twice(s.gain1[rows, :])
        normed = s.x_t[rows, :].astype(F32) * s.root1[0:1]
        grad_x[:, rows] = (s.resid[rows, :] + s.root1[0:1] * (scaled - normed * inner)).T

    loop(4, last_back)

    for step in range(7):
        if step % 2 == 0 and dp_attn.phase < 5:
            dp_attn.advance()
        gain_copies[step].wait_recv()
        total = s.gain_parts[step] + s.gain_parts[7 + step]
        if step < 6:
            s.gain_parts[step + 1] = total
            following = links.send(s.gain_parts.at[step + 1], s.gain_parts.at[8 + step], GAIN_ORDER[step + 1])
            gain_copies.append(following)
        else:
            out_g1[...] = total[0:1]
            out_g2[...] = total[1:2]
            out_gq[...] = total[2:3, :128]
            out_gk[...] = total[2:3, 128:256]
    out_q[...] = s.sums[:, pl.ds(0, 512)]
    out_k[...] = s.sums[:, pl.ds(512, 256)]
    out_v[...] = s.sums[:, pl.ds(768, 256)]
    out_o[...] = s.sums[:, pl.ds(1024, 512)].T
    out_g[...] = s.sums[:, pl.ds(1536, 768)]
    out_u[...] = s.sums[:, pl.ds(2304, 768)]
    out_d[...] = s.sums[:, pl.ds(3072, 768)].T

    for copy in gain_copies:
        copy.wait_send()
    for exchange in (gather_h1, gather_da, sum_mlp, sum_dh1, dp_mlp, dp_attn):
        exchange.drain()


def shards(
    tokens,
    doc_starts,
    cotangent,
    w_query,
    key_matrix,
    value_matrix,
    w_out,
    w_gate,
    w_up,
    w_down,
    gain_attn,
    gain_mlp,
    gain_query,
    gain_key,
):
    frequency = ROPE_BASE ** (-(np.arange(64, dtype=np.float64) * 2.0) / HEAD)
    frequency = jnp.asarray(np.broadcast_to(frequency[:, None], (64, 128)).astype(np.float32))
    vmem = pl.BlockSpec(memory_space=pltpu.VMEM)
    hbm = pl.BlockSpec(memory_space=pl.ANY)
    smem = pl.BlockSpec(memory_space=pltpu.SMEM)

    def shaped(*shape, kind=F32):
        return jax.ShapeDtypeStruct(shape, kind)

    outs = pl.pallas_call(
        layer_kernel,
        out_shape=(
            shaped(256, 1024, kind=BF16),
            shaped(256, 1024),
            shaped(32, 512),
            shaped(32, 256),
            shaped(32, 256),
            shaped(512, 32),
            shaped(32, 768),
            shaped(32, 768),
            shaped(768, 32),
            shaped(1, 1024),
            shaped(1, 1024),
            shaped(1, 128),
            shaped(1, 128),
        ),
        in_specs=[vmem, smem, vmem] + [hbm] * 7 + [vmem] * 5,
        out_specs=(vmem,) * 13,
        scratch_shapes=[pltpu.VMEM(shape, kind) for _, shape, kind in SCRATCH]
        + [
            pltpu.SemaphoreType.DMA((2, SEMAPHORES)),
            pltpu.SemaphoreType.DMA((8,)),
            pltpu.SemaphoreType.REGULAR((5,)),
        ],
        compiler_params=pltpu.CompilerParams(
            collective_id=0, has_side_effects=True, vmem_limit_bytes=64 * 2**20 - 2**16
        ),
        cost_estimate=pl.CostEstimate(flops=32 * 10**9, bytes_accessed=2**24, transcendentals=2**22),
        name="layer",
    )(
        tokens.reshape(256, 1024),
        doc_starts,
        cotangent.reshape(256, 1024),
        w_query,
        key_matrix,
        value_matrix,
        w_out,
        w_gate.reshape(4, 4, 64, 768),
        w_up.reshape(4, 4, 64, 768),
        w_down,
        gain_attn.reshape(1, 1024),
        gain_mlp.reshape(1, 1024),
        gain_query.reshape(1, 128),
        gain_key.reshape(1, 128),
        frequency,
    )
    return (
        outs[0].reshape(1, 256, 1024),
        outs[1].reshape(1, 256, 1024),
        *outs[2:9],
        *(gain.reshape(-1) for gain in outs[9:]),
    )


def solution(mesh):
    in_specs = (
        P("dp", "tensor", None),
        P("dp", None),
        P("dp", "tensor", None),
        P(None, "tensor"),
        P(None, "tensor"),
        P(None, "tensor"),
        P("tensor", None),
        P(None, "tensor"),
        P(None, "tensor"),
        P("tensor", None),
        P(),
        P(),
        P(),
        P(),
    )
    out_specs = (
        P("dp", "tensor", None),
        P("dp", "tensor", None),
        P("dp", "tensor"),
        P("dp", "tensor"),
        P("dp", "tensor"),
        P("tensor", "dp"),
        P("dp", "tensor"),
        P("dp", "tensor"),
        P("tensor", "dp"),
        P(),
        P(),
        P(),
        P(),
    )
    return jax.shard_map(shards, mesh=mesh, in_specs=in_specs, out_specs=out_specs, check_vma=False)
```

time: 1520 us -> 178 us (0.12)
  waiting for transfers between devices: 1230 us -> 0 us
  Pallas kernels: 0 us -> 165 us
  matrix products: 116 us -> 0 us
  blocking collectives: 68 us -> 0 us
  other arithmetic: 54.5 us -> 0 us
    reduce_scatter x11 -> x0, waiting for transfers between devices: 1150 us -> none  [the longest x1 161 us: shards(): lax.psum_scatter(grad_w_up.astype(jnp.bfloat16), 'dp', scatter_dimension=...]
    pallas_call x0 -> x1, Pallas kernels: none -> 165 us  [shards(): pl.pallas_call(layer_kernel, out_shape=(shaped(256, 1024, kind=BF16), sha...]
    dot_general x27 -> x0, matrix products: 116 us -> none  [the longest x7 27 us: outer_rows(): lax.dot_general(left_side, right_side, (((0,), (0,)), ((), ())), preferre...]
    all_gather x4 -> x0, waiting for transfers between devices: 77.7 us -> none  [the longest x1 25.6 us: shards(): lax.all_gather(normed_mlp, 'tensor', axis=1, tiled=True)]
    psum x1 -> x0, blocking collectives: 68 us -> none  [shards(): lax.psum((grad_gain_attn, grad_gain_mlp, grad_gain_query, grad_gain_key),...]
    convert_element_type x14 -> x0, other arithmetic: 26.8 us -> none  [the longest x7 9.79 us: shards(): summed_weights = (lax.psum_scatter(grad_w_query.astype(jnp.bfloat16), 'dp...]
    reduce_sum x9 -> x0, other arithmetic: 16.5 us -> none  [the longest x1 8.16 us: attend(): row_total = jnp.sum(weights, axis=-1, keepdims=True)]
  transfers between devices with their start and end apart: 15 -> 0, of which waited for: 14 -> 0; matrix products, arithmetic and copies ran while one was open for 7% -> 0% of each run, Pallas kernels for 0% -> 0%
where the time goes in v2:
time: 178 us
  Pallas kernels  165 us (93%)
  local copies, waits for them, and re-layouts  11.8 us (7%)
    pallas_call x1, Pallas kernels, shards(): pl.pallas_call(layer_kernel, out_shape=(shaped(256, 1024, kind=BF16), sha...  165 us
    unnamed x33, local copies, waits for them, and re-layouts  11.8 us

profile of v2, /device:TPU:6, one launch (start us, length us, event | category | flops | bytes accessed | tf_op | source)
XLA Modules:
  0.0 177.7 jit_solution(11004318577362558540)
XLA Ops:
  0.7 165.2 %layer.1 = (bf16[256,1024]{1,0:T(8,128)(2,1)}, f32[256,1024]{1,0:T(8,128)}, f32[32,512]{1,0:T(8,128)}, f32[32,256]{1,0:T(8,128)}, f32[32,256]{1,0:T(8,128)}, /*i...) custom-call(bf16[256,1024]{1,0:T(8,128)(2,1)} %bitcast.20, ...), custom_call_target="tpu_custom_call" | custom-call | flops 32000000000 | bytes 16777216 | tf_op jit(solution)/shard_map/layer/pallas_call | solution.py:873
  165.8 0.0 copy-start
  165.8 1.8 copy.28
  167.6 1.8 %copy.29 = f32[768,32]{0,1:T(8,128)} copy(f32[768,32]{1,0:T(8,128)} %get-tuple-element.47) | data formatting | bytes 196608
  169.4 0.0 copy-start.5
  169.4 0.0 copy-start.4
  169.4 0.0 copy-start.2
  169.4 0.0 copy-start.1
  169.4 1.9 %copy.41 = bf16[1,256,1024]{2,1,0:T(8,128)(2,1)} copy(bf16[1,256,1024]{2,1,0:T(8,128)(2,1)} %bitcast.15) | data formatting | bytes 1048576
  171.3 0.0 copy-done
  171.3 0.0 copy-start.7
  171.3 0.0 copy-start.6
  171.3 0.0 copy-start.8
  171.4 1.0 copy.42
  172.3 0.0 copy-done.3
  172.3 0.6 copy.43
  173.0 0.0 copy-done.5
  173.0 0.6 copy.44
  173.6 0.0 copy-done.4
  173.6 0.6 copy.45
  174.2 0.0 copy-done.2
  174.2 0.6 copy.46
  174.8 0.0 copy-done.1
  174.8 0.6 copy.47
  175.5 0.0 copy-done.7
  175.5 0.6 copy.48
  176.1 0.0 copy-done.6
  176.1 0.6 copy.49
  176.7 0.0 copy-done.9
  176.7 0.5 copy.50
  177.2 0.0 copy-done.8
  177.2 0.5 copy.51
  (2 shorter events, 0.0 us)
Async XLA Ops:
  165.8 5.5 %copy-start = (f32[256,1024]{1,0:T(8,128)S(1)}, f32[256,1024]{1,0:T(8,128)}, u32[]{:S(2)}) copy-start(f32[256,1024]{1,0:T(8,128)} %get-tuple-element.27) | copy-start | bytes 3145732
  169.4 2.9 %copy-start.3 = (f32[32,512]{1,0:T(8,128)S(1)}, f32[32,512]{1,0:T(8,128)}, u32[]{:S(2)}) copy-start(f32[32,512]{1,0:T(8,128)} %get-tuple-element.67) | copy-start | bytes 196612
  169.4 3.6 %copy-start.5 = (f32[32,256]{1,0:T(8,128)S(1)}, f32[32,256]{1,0:T(8,128)}, u32[]{:S(2)}) copy-start(f32[32,256]{1,0:T(8,128)} %get-tuple-element.68) | copy-start | bytes 98308
  169.4 4.2 %copy-start.4 = (f32[32,256]{1,0:T(8,128)S(1)}, f32[32,256]{1,0:T(8,128)}, u32[]{:S(2)}) copy-start(f32[32,256]{1,0:T(8,128)} %get-tuple-element.69) | copy-start | bytes 98308
  169.4 4.8 %copy-start.2 = (f32[32,768]{1,0:T(8,128)S(1)}, f32[32,768]{1,0:T(8,128)}, u32[]{:S(2)}) copy-start(f32[32,768]{1,0:T(8,128)} %get-tuple-element.71) | copy-start | bytes 294916
  169.4 5.4 %copy-start.1 = (f32[32,768]{1,0:T(8,128)S(1)}, f32[32,768]{1,0:T(8,128)}, u32[]{:S(2)}) copy-start(f32[32,768]{1,0:T(8,128)} %get-tuple-element.72) | copy-start | bytes 294916
  171.3 4.2 %copy-start.7 = (f32[1,1024]{1,0:T(1,128)S(1)}, f32[1,1024]{1,0:T(1,128)}, u32[]{:S(2)}) copy-start(f32[1,1024]{1,0:T(1,128)} %get-tuple-element.35) | copy-start | bytes 12292
  171.3 4.7 %copy-start.6 = (f32[1,1024]{1,0:T(1,128)S(1)}, f32[1,1024]{1,0:T(1,128)}, u32[]{:S(2)}) copy-start(f32[1,1024]{1,0:T(1,128)} %get-tuple-element.36) | copy-start | bytes 12292
  171.3 5.3 %copy-start.9 = (f32[1,128]{1,0:T(1,128)S(1)}, f32[1,128]{1,0:T(1,128)}, u32[]{:S(2)}) copy-start(f32[1,128]{1,0:T(1,128)} %get-tuple-element.37) | copy-start | bytes 1540
  171.3 5.8 %copy-start.8 = (f32[1,128]{1,0:T(1,128)S(1)}, f32[1,128]{1,0:T(1,128)}, u32[]{:S(2)}) copy-start(f32[1,128]{1,0:T(1,128)} %get-tuple-element.38) | copy-start | bytes 1540

commit v3 on v2

--- a/solution.py
+++ b/solution.py
@@ -18,8 +18,9 @@
 QUERY_SCALE = math.log2(math.e) / math.sqrt(HEAD)
 PARTNERS = ("core", "far", "y1", "y2", "z1", "z2", "x")
 ORDERS = (("y1", "y2", "z1", "z2"), ("y2", "y1", "z2", "z1"), ("z1", "z2", "y1", "y2"), ("z2", "z1", "y2", "y1"))
-MLP_WIDTHS = (640, 640, 512, 512)
-ATTN_WIDTHS = (384, 384, 384, 384)
+MLP_STREAMS = ((640, 0, 0), (640, 4, 0), (512, 8, 0), (512, 12, 0))
+HIGH_STREAMS = ((256, 10, 0), (256, 10, 256), (256, 14, 0), (256, 14, 256))
+LOW_STREAMS = ((128, 0, 0), (128, 0, 128), (128, 0, 256), (128, 0, 384))
 GAIN_ORDER = ("core", "y1", "y2", "z1", "z2", "x", "far")
 
 SCRATCH = (
@@ -59,7 +60,7 @@
     ("gain_k_sum", (128, 256), F32),
     ("root1", (8, 256), F32),
     ("root2", (8, 256), F32),
-    ("acc_o", (144, 512), F32),
+    ("acc_o", (3, 2, 144, 512), F32),
     ("acc_q", (128, 512), F32),
     ("keep_far", (1024, 256), F32),
     ("keep_own", (1024, 256), F32),
@@ -74,9 +75,11 @@
     ("mlp_far_in", (1024, 256), BF16),
     ("mlp_halves", (16, 4, 64, 640), BF16),
     ("sums", (32, 3840), F32),
+    ("result", (256, 1024), F32),
+    ("stage", (256, 1024), BF16),
     ("gain_parts", (14, 8, 1024), F32),
 )
-SEMAPHORES = 120
+SEMAPHORES = 140
 
 
 class Box:
@@ -229,33 +232,41 @@
 
 
 class DpSum:
-    def __init__(self, links, source, widths, bufs, out, out_first):
-        self.links, self.source, self.bufs, self.out, self.out_first = links, source, bufs, out, out_first
-        self.widths = widths
-        self.first = [sum(widths[:k]) for k in range(4)]
+    def __init__(self, links, source, source_first, streams, bufs, out, out_first):
+        self.links, self.source, self.bufs, self.out = links, source, bufs, out
+        self.streams = streams
+        before = [sum(w for w, _, _ in streams[:k]) for k in range(4)]
+        self.source_first = [source_first + first for first in before]
+        self.out_first = [out_first + first for first in before]
         self.phase = -1
         self.flying = [[], [], [], []]
         self.sent = []
 
+    def spot(self, stream, slot, *rest):
+        w, at, column = self.streams[stream]
+        lead = pl.ds(at + slot.start, slot.size) if isinstance(slot, pl.Slice) else at + slot
+        return (lead, *rest, pl.ds(column, w))
+
     def held(self, stream, phase):
-        w = self.widths[stream]
-        at = 4 * stream
+        every = slice(None)
         if phase == 0:
-            return self.bufs.at[pl.ds(at, 2), :, :, pl.ds(0, w)]
-        if phase == 1:
-            return self.bufs.at[at + 2, :, :, pl.ds(0, w)]
-        if phase == 2:
-            return self.bufs.at[at + 3, pl.ds(0, 2), :, pl.ds(0, w)]
-        if phase == 3:
-            return self.bufs.at[at + 3, 2, :, pl.ds(0, w)]
-        return self.bufs.at[at + 3, 3, pl.ds(0, 32), pl.ds(0, w)]
+            spot = self.spot(stream, pl.ds(0, 2), every, every)
+        elif phase == 1:
+            spot = self.spot(stream, 2, every, every)
+        elif phase == 2:
+            spot = self.spot(stream, 3, pl.ds(0, 2), every)
+        elif phase == 3:
+            spot = self.spot(stream, 3, 2, every)
+        else:
+            spot = self.spot(stream, 3, 3, pl.ds(0, 32))
+        return self.bufs.at[spot]
 
     def begin(self, stream, phase):
         place, send = self.links.place, self.links.send
         order = ORDERS[stream]
         into = self.held(stream, phase)
         if phase == 4:
-            theirs = self.held(stream, 3).at[span(1 - place.x, 32)]
+            theirs = self.bufs.at[self.spot(stream, 3, 2, span(1 - place.x, 32))]
             return [send(theirs, into, "x")]
         name = order[phase]
         if phase in (1, 3):
@@ -266,39 +277,41 @@
             if phase == 2:
                 source = self.held(stream, 1).at[at]
             else:
-                columns = pl.ds(self.first[stream], self.widths[stream])
+                columns = pl.ds(self.source_first[stream], self.streams[stream][0])
                 source = self.source.at[:, at, :, columns] if name[0] == "y" else self.source.at[at, :, :, columns]
             copies.append(send(source, into.at[j], name))
         return copies
 
     def finish(self, stream, phase):
-        place = self.links.place
-        order, first, w = ORDERS[stream], self.first[stream], self.widths[stream]
-        at = 4 * stream
-        bufs = self.bufs
+        place, spot, bufs = self.links.place, self.spot, self.bufs
+        order, w = ORDERS[stream], self.streams[stream][0]
+        every = slice(None)
         for copy in self.flying[stream]:
             copy.wait_recv()
         if phase == 4:
-            mine = bufs[at + 3, 2, span(place.x, 32), pl.ds(0, w)].astype(F32)
-            columns = pl.ds(self.out_first + first, w)
-            self.out[:, columns] = bufs[at + 3, 3, pl.ds(0, 32), pl.ds(0, w)].astype(F32) + mine
+            mine = bufs[spot(stream, 3, 2, span(place.x, 32))].astype(F32)
+            columns = pl.ds(self.out_first[stream], w)
+            self.out[:, columns] = bufs[spot(stream, 3, 3, pl.ds(0, 32))].astype(F32) + mine
         elif phase == 3:
-            bufs[at + 3, 2, :, pl.ds(0, w)] += bufs[at + 3, 0, :, pl.ds(0, w)]
+            bufs[spot(stream, 3, 2, every)] += bufs[spot(stream, 3, 0, every)]
         elif phase == 1:
             for k in range(4):
-                bufs[at + 2, k, :, pl.ds(0, w)] += bufs[at, k, :, pl.ds(0, w)]
+                bufs[spot(stream, 2, k, every)] += bufs[spot(stream, 0, k, every)]
         else:
             name = order[phase]
             mine = place.y if name[0] == "y" else place.z
             for j, own in enumerate((mine, step_of(order[phase + 1], mine))):
                 if phase == 2:
-                    bufs[at + 3, j, :, pl.ds(0, w)] += bufs[at + 2, own, :, pl.ds(0, w)]
+                    bufs[spot(stream, 3, j, every)] += bufs[spot(stream, 2, own, every)]
                     continue
                 for k in range(4):
                     lead = (k, own) if name[0] == "y" else (own, k)
-                    bufs[at + j, k, :, pl.ds(0, w)] += self.source[(*lead, slice(None), pl.ds(first, w))]
+                    kept = self.source[(*lead, every, pl.ds(self.source_first[stream], w))]
+                    bufs[spot(stream, j, k, every)] += kept
 
     def advance(self):
+        if self.phase == 5:
+            return
         for stream in range(4):
             if self.phase >= 0:
                 self.finish(stream, self.phase)
@@ -307,8 +320,43 @@
                 self.flying[stream] = self.begin(stream, self.phase + 1)
         self.phase += 1
 
+    def complete(self):
+        while self.phase < 5:
+            self.advance()
+
     def drain(self):
         for copy in self.sent:
+            copy.wait_send()
+
+
+class GainSum:
+    def __init__(self, links, parts):
+        self.links, self.parts, self.copies, self.step = links, parts, [], 0
+        self.begin()
+
+    def begin(self):
+        step = self.step
+        self.copies.append(self.links.send(self.parts.at[step], self.parts.at[7 + step], GAIN_ORDER[step]))
+
+    def advance(self):
+        if self.step == 7:
+            return
+        step = self.step
+        self.copies[step].wait_recv()
+        total = self.parts[step] + self.parts[7 + step]
+        self.step += 1
+        if self.step < 7:
+            self.parts[self.step] = total
+            self.begin()
+        else:
+            self.total = total
+
+    def complete(self):
+        while self.step < 7:
+            self.advance()
+
+    def drain(self):
+        for copy in self.copies:
             copy.wait_send()
 
 
@@ -331,7 +379,7 @@
 
 def layer_kernel(
     x, starts, dy, wq, wk, wv, wo, wg, wu, wd, g1, g2, gq, gk, frequency,
-    out, grad_x, out_q, out_k, out_v, out_o, out_g, out_u, out_d, out_g1, out_g2, out_gq, out_gk,
+    out, grad_x, out_sums, out_g1, out_g2, out_gq, out_gk,
     *scratch,
 ):
     s = Box()
@@ -345,7 +393,6 @@
     barrier = pltpu.get_barrier_semaphore()
     for name in PARTNERS:
         pl.semaphore_signal(barrier, inc=1, device_id=place.device(name), device_id_type=MESH)
-    pl.semaphore_wait(barrier, len(PARTNERS))
 
     loads = []
 
@@ -354,32 +401,37 @@
         copy.start()
         loads.append(copy)
 
-    load(wq, s.w_qkv.at[:, pl.ds(0, 512)])
-    load(wk, s.w_qkv.at[:, pl.ds(512, 256)])
-    load(wv, s.w_qkv.at[:, pl.ds(768, 256)])
+    for g in range(2):
+        load(wq.at[:, pl.ds(256 * g, 256)], s.w_qkv.at[:, pl.ds(512 * g, 256)])
+        load(wk.at[:, pl.ds(128 * g, 128)], s.w_qkv.at[:, pl.ds(512 * g + 256, 128)])
+        load(wv.at[:, pl.ds(128 * g, 128)], s.w_qkv.at[:, pl.ds(512 * g + 384, 128)])
     load(wo, s.h2.at[pl.ds(0, 512)])
     load(wg, s.mlp_mix.at[:, :, :, pl.ds(0, 768)])
     load(wu, s.mlp_mix.at[:, :, :, pl.ds(768, 768)])
     load(wd, s.w_down)
+    load(dy, s.da.at[pl.ds(0, 256)])
 
     def first_norm(i):
         rows = span(i, 64)
         xs = x[rows, :].astype(F32)
         root = lax.rsqrt(jnp.mean(xs * xs, axis=1, keepdims=True) + EPSILON)
-        out[rows, :] = (xs * root * g1[...]).astype(BF16)
+        s.stage[rows, :] = (xs * root * g1[...]).astype(BF16)
 
     loop(4, first_norm)
     gather_h1 = Gather(links, lambda half, b: s.h1.at[pl.ds(512 * half, 512), span(b)])
     for half in range(2):
         for j in range(2):
-            s.h1[pl.ds(512 * half + 256 * j, 256), span(me)] = out[:, pl.ds(512 * half + 256 * j, 256)].T
+            s.h1[pl.ds(512 * half + 256 * j, 256), span(me)] = s.stage[:, pl.ds(512 * half + 256 * j, 256)].T
+        if half == 0:
+            pl.semaphore_wait(barrier, len(PARTNERS))
         gather_h1.send(half)
 
     def dy_in(i):
-        s.attn_mix[i, :, :, span(me)] = dy[:, span(i)].T.reshape(4, 64, BLOCK)
-
+        s.attn_mix[i, :, :, span(me)] = s.da[pl.ds(0, 256), span(i)].T.reshape(4, 64, BLOCK)
+
+    loads[10].wait()
     loop(4, dy_in)
-    for k in range(3):
+    for k in range(6):
         loads[k].wait()
 
     def turn_qkv(i):
@@ -423,21 +475,21 @@
     root = lax.rsqrt(jnp.sum(square, axis=0, keepdims=True) / 1024.0 + EPSILON)
     s.root1[...] = jnp.broadcast_to(root, (8, BLOCK))
 
-    loads[3].wait()
+    loads[6].wait()
 
     def turn_out(i):
         s.attn_mix[i, :, :, pl.ds(1024, 512)] = s.h2[pl.ds(0, 512), span(i)].T.reshape(4, 64, 512)
 
     loop(4, turn_out)
-    loads[4].wait()
-    loads[5].wait()
+    loads[7].wait()
+    loads[8].wait()
 
     def turn_gu(i):
         for z in range(4):
             s.t_gu[span(i), pl.ds(256 * z, 256)] = s.mlp_mix[z, :, :, span(i)].reshape(256, 256).T
 
     loop(6, turn_gu)
-    loads[6].wait()
+    loads[9].wait()
 
     def turn_down(i):
         s.mlp_mix[i, :, :, pl.ds(1536, 768)] = s.w_down[:, span(i)].T.reshape(4, 64, 768)
@@ -447,30 +499,54 @@
     def project(b):
         columns = span(b)
         cosine, sine = s.cosine[:, columns], s.sine[:, columns]
+        query_gain = twice(s.gain_q[...] * QUERY_SCALE)
+        key_gain = twice(s.gain_k[...])
         for g in range(2):
-            raw = nn(s.t_qkv[pl.ds(256 * g, 256), :], s.h1[:, columns])
-            gain = twice(s.gain_q[...] * QUERY_SCALE)
+            raw = nn(s.t_qkv[pl.ds(512 * g, 256), :], s.h1[:, columns])
             for k in range(2):
-                head = 2 * g + k
-                normed, root, turned = head_forward(raw[128 * k : 128 * k + 128], gain, cosine, sine)
+                head = 3 * g + k
+                normed, root, turned = head_forward(raw[128 * k : 128 * k + 128], query_gain, cosine, sine)
                 s.norm_qk[pl.ds(128 * head, 128), columns] = normed.astype(BF16)
                 s.root_qk[pl.ds(head, 1), columns] = root
                 s.qs[g, b, :, pl.ds(256 * k, 256)] = turned.astype(BF16)
-        raw = nn(s.t_qkv[pl.ds(512, 256), :], s.h1[:, columns])
-        gain = twice(s.gain_k[...])
-        for g in range(2):
-            normed, root, turned = head_forward(raw[128 * g : 128 * g + 128], gain, cosine, sine)
-            s.norm_qk[pl.ds(512 + 128 * g, 128), columns] = normed.astype(BF16)
-            s.root_qk[pl.ds(4 + g, 1), columns] = root
+            raw = nn(s.t_qkv[pl.ds(512 * g + 256, 256), :], s.h1[:, columns])
+            normed, root, turned = head_forward(raw[:128], key_gain, cosine, sine)
+            s.norm_qk[pl.ds(384 * g + 256, 128), columns] = normed.astype(BF16)
+            s.root_qk[pl.ds(3 * g + 2, 1), columns] = root
             s.ks_t[pl.ds(128 * g, 128), columns] = turned.astype(BF16)
             s.ks[g, columns, :] = turned.astype(BF16).T
-        raw = nn(s.t_qkv[pl.ds(768, 256), :], s.h1[:, columns]).astype(BF16)
-        for g in range(2):
-            s.v_t[g, pl.ds(0, 128), columns] = raw[128 * g : 128 * g + 128]
-            s.v[g, columns, :] = raw[128 * g : 128 * g + 128].T
-
+            values = raw[128:].astype(BF16)
+            s.v_t[g, pl.ds(0, 128), columns] = values
+            s.v[g, columns, :] = values.T
+
+    def attend_to(qb, slot, first, last):
+        def group(g):
+            def keys(kb):
+                at = qb * (qb + 1) // 2 + kb
+                scores = nn(s.ks[g, span(kb), :], s.qs[g, qb])
+                weights = jnp.exp2(scores).astype(BF16) * twice(s.mask[at])
+                s.p[g * 10 + at] = weights.reshape(4, 64, 512)
+                s.acc_o[slot, g] += nn(s.v_t[g, :, span(kb)], weights)
+
+            lax.fori_loop(first, last, lambda kb, carry: (keys(kb), carry)[1], 0)
+
+        loop(2, group)
+
+    def attend_end(qb, slot):
+        def group(g):
+            inverse = 1.0 / s.acc_o[slot, g, pl.ds(128, 8), :]
+            s.inv[g, qb] = inverse
+            attended = (s.acc_o[slot, g, pl.ds(0, 128), :] * inverse[0:1]).astype(BF16)
+            rows = pl.multiple_of(g * 256, 256)
+            s.ob[pl.ds(rows, 128), span(qb)] = attended[:, :256]
+            s.ob[pl.ds(rows + 128, 128), span(qb)] = attended[:, 256:]
+
+        loop(2, group)
+
+    s.acc_o[pl.ds(0, 2)] = jnp.zeros((2, 2, 144, 512), F32)
     gather_h1.near_ready()
     loop(2, lambda i: project(place.far * 2 + i))
+    loop(2, lambda i: attend_to(place.far * 2 + i, i, place.far * 2, place.far * 2 + i + 1))
     gather_h1.pass_on()
     gather_dy = Gather(links, lambda half, b: s.attn_mix.at[pl.ds(2 * half, 2), :, :, span(b)])
     gather_dy.send(0)
@@ -478,32 +554,11 @@
     gather_h1.far_ready()
     loop(2, lambda i: project((1 - place.far) * 2 + i))
 
-    def attend(qb):
-        def group(g):
-            s.acc_o[...] = jnp.zeros((144, 512), F32)
-
-            def keys(kb):
-                at = qb * (qb + 1) // 2 + kb
-                scores = nn(s.ks[g, span(kb), :], s.qs[g, qb])
-                weights = jnp.exp2(scores).astype(BF16) * twice(s.mask[at])
-                s.p[g * 10 + at] = weights.reshape(4, 64, 512)
-                s.acc_o[...] += nn(s.v_t[g, :, span(kb)], weights)
-
-            loop(qb + 1, keys)
-            inverse = 1.0 / s.acc_o[pl.ds(128, 8), :]
-            s.inv[g, qb] = inverse
-            attended = (s.acc_o[pl.ds(0, 128), :] * inverse[0:1]).astype(BF16)
-            rows = pl.multiple_of(g * 256, 256)
-            s.ob[pl.ds(rows, 128), span(qb)] = attended[:, :256]
-            s.ob[pl.ds(rows + 128, 128), span(qb)] = attended[:, 256:]
-
-        loop(2, group)
-
-    def out_product(b, store):
+    def out_product(b, store, first=0, last=4):
         def body(i):
             store(i, nn(s.attn_mix[i, :, :, pl.ds(1024, 512)].reshape(256, 512), s.ob[:, span(b)]))
 
-        loop(4, body)
+        lax.fori_loop(first, last, lambda i, carry: (body(i), carry)[1], 0)
 
     def to(ref, index=None):
         def store(i, values):
@@ -515,18 +570,28 @@
         return store
 
     sum_attn = Reduce(links, s.sib_out, s.sib_in, s.far_out, s.far_in)
-    attend(across_sib)
+
+    def attend_far(qb):
+        s.acc_o[2] = jnp.zeros((2, 144, 512), F32)
+        attend_to(qb, 2, 0, qb + 1)
+        attend_end(qb, 2)
+
+    attend_far(across_sib)
     out_product(across_sib, to(s.sib_out, 0))
     sum_attn.to_sibling(0)
-    attend(across)
-    out_product(across, to(s.keep_far))
+    attend_far(across)
     for half in range(2):
+        out_product(across, to(s.keep_far), 2 * half, 2 * half + 2)
         sum_attn.make_far(s.keep_far, half)
         sum_attn.send_far(half)
-    attend(sib)
+
+    def attend_own(i):
+        attend_to(place.far * 2 + i, i, 0, place.far * 2)
+        attend_end(place.far * 2 + i, i)
+
+    loop(2, attend_own)
     out_product(sib, to(s.sib_out, 1))
     sum_attn.to_sibling(1)
-    attend(me)
     out_product(me, to(s.keep_own))
     gather_dy.near_ready()
     gather_dy.pass_on()
@@ -572,11 +637,11 @@
 
         loop(3, body)
 
-    def feed_back(b, store):
+    def feed_back(b, store, first=0, last=4):
         def body(i):
             store(i, nn(s.mlp_mix[i, :, :, pl.ds(0, 1536)].reshape(256, 1536), s.dgu[:, span(b)]))
 
-        loop(4, body)
+        lax.fori_loop(first, last, lambda i, carry: (body(i), carry)[1], 0)
 
     def mlp_product(b, store):
         def body(i):
@@ -597,8 +662,8 @@
     feed_back(across_sib, to(s.sib_out, 0))
     sum_dh2.to_sibling(0)
     feed(across)
-    feed_back(across, to(s.keep_far))
     for half in range(2):
+        feed_back(across, to(s.keep_far), 2 * half, 2 * half + 2)
         sum_dh2.make_far(s.keep_far, half)
         sum_dh2.send_far(half)
 
@@ -628,9 +693,8 @@
 
     loop(4, gate_up_grad)
     gather_h2.drain()
-    again = pltpu.make_async_copy(wo, s.h2.at[pl.ds(0, 512)], load_sems.at[7])
-    again.start()
-    dp_mlp = DpSum(links, s.mlp_mix, MLP_WIDTHS, s.mlp_halves, s.sums, 1536)
+    load(wo, s.h2.at[pl.ds(0, 512)])
+    dp_mlp = DpSum(links, s.mlp_mix, 0, MLP_STREAMS, s.mlp_halves, s.sums, 1536)
     dp_mlp.advance()
 
     sum_dh2.arrive()
@@ -661,11 +725,11 @@
         gather_da.send(half)
     sum_dh2.drain()
     s.gain_parts[0, 1:2, :] = jnp.sum(s.gain_sum[...].T, axis=0, keepdims=True)
-    dp_mlp.advance()
+    s.gain_sum[...] = jnp.zeros((1024, 128), F32)
 
     s.keep_own[...] = jnp.zeros((1024, 256), F32)
     s.keep_far[...] = jnp.zeros((1024, 256), F32)
-    again.wait()
+    loads[11].wait()
 
     def out_back(b):
         def body(g):
@@ -678,121 +742,149 @@
 
         loop(2, body)
 
-    gather_da.near_ready()
-    loop(2, lambda i: out_back(place.far * 2 + i))
-    gather_da.pass_on()
-    for half in range(2):
-        sum_mlp.send_far(half)
-    gather_da.far_ready()
-    loop(2, lambda i: out_back((1 - place.far) * 2 + i))
-
-    def out_grad(i):
-        s.attn_mix[i, :, :, pl.ds(1024, 512)] = nt(s.da[span(i), :], s.ob[...]).astype(BF16).reshape(4, 64, 512)
-
-    loop(4, out_grad)
-    dp_mlp.advance()
-
-    def attend_back(qb):
+    def attend_back(qb, g):
         columns = span(qb)
         cosine, sine = s.cosine[:, columns], s.sine[:, columns]
         gain = twice(s.gain_q[...])
-        for g in range(2):
-            s.acc_q[...] = jnp.zeros((128, 512), F32)
-
-            def keys(kb, g=g):
-                at = g * 10 + qb * (qb + 1) // 2 + kb
-                rows = span(kb)
-                grads = s.t_gu[span(g * 4 + qb, 128), pl.ds(0, 512)]
-                weights = s.p[at].reshape(256, 512)
-                slope = nn(s.v[g, rows, :], grads) - s.inner[g, qb][0:1]
-                ds = (weights.astype(F32) * slope).astype(BF16)
-                s.keep_own[rows, pl.ds(128 * g, 128)] += nt(weights, grads)
-                s.keep_far[rows, pl.ds(128 * g, 128)] += nt(ds, s.qs[g, qb])
-                s.acc_q[...] += nn(s.ks_t[pl.ds(128 * g, 128), rows], ds)
-
-            loop(qb + 1, keys)
-            for k in range(2):
-                head = 2 * g + k
-                grad, gain_part = head_backward(
-                    s.acc_q[:, pl.ds(256 * k, 256)] * (1.0 / math.sqrt(HEAD)),
-                    s.norm_qk[pl.ds(128 * head, 128), columns].astype(F32),
-                    s.root_qk[pl.ds(head, 1), columns],
-                    gain,
-                    cosine,
-                    sine,
-                )
-                s.t_qkv[pl.ds(128 * head, 128), columns] = grad.astype(BF16)
-                s.gain_q_sum[...] += gain_part
-
-    loop(2, attend_back)
-    dp_mlp.advance()
-    loop(2, lambda i: attend_back(2 + i))
-    dp_mlp.advance()
-
-    for k, name in enumerate(PARTNERS[2:]):
-        pl.semaphore_signal(ready.at[k], inc=1, device_id=place.device(name), device_id_type=MESH)
-
-    def key_back(b):
-        columns = span(b)
-        cosine, sine = s.cosine[:, columns], s.sine[:, columns]
-        gain = twice(s.gain_k[...])
-        for g in range(2):
+        s.acc_q[...] = jnp.zeros((128, 512), F32)
+
+        def keys(kb):
+            at = g * 10 + qb * (qb + 1) // 2 + kb
+            rows = span(kb)
+            grads = s.t_gu[span(g * 4 + qb, 128), pl.ds(0, 512)]
+            weights = s.p[at].reshape(256, 512)
+            slope = nn(s.v[g, rows, :], grads) - s.inner[g, qb][0:1]
+            ds = (weights.astype(F32) * slope).astype(BF16)
+            s.keep_own[rows, pl.ds(128 * g, 128)] += nt(weights, grads)
+            s.keep_far[rows, pl.ds(128 * g, 128)] += nt(ds, s.qs[g, qb])
+            s.acc_q[...] += nn(s.ks_t[pl.ds(128 * g, 128), rows], ds)
+
+        loop(qb + 1, keys)
+        for k in range(2):
+            head = 3 * g + k
             grad, gain_part = head_backward(
-                s.keep_far[columns, pl.ds(128 * g, 128)].T * math.log(2.0),
-                s.norm_qk[pl.ds(512 + 128 * g, 128), columns].astype(F32),
-                s.root_qk[pl.ds(4 + g, 1), columns],
+                s.acc_q[:, pl.ds(256 * k, 256)] * (1.0 / math.sqrt(HEAD)),
+                s.norm_qk[pl.ds(128 * head, 128), columns].astype(F32),
+                s.root_qk[pl.ds(head, 1), columns],
                 gain,
                 cosine,
                 sine,
             )
-            s.t_qkv[pl.ds(512 + 128 * g, 128), columns] = grad.astype(BF16)
+            s.t_qkv[pl.ds(512 * g + 128 * k, 128), columns] = grad.astype(BF16)
+            s.gain_q_sum[...] += gain_part
+
+    def key_back(g):
+        gain = twice(s.gain_k[...])
+
+        def body(b):
+            columns = span(b)
+            grad, gain_part = head_backward(
+                s.keep_far[columns, pl.ds(128 * g, 128)].T * math.log(2.0),
+                s.norm_qk[pl.ds(384 * g + 256, 128), columns].astype(F32),
+                s.root_qk[pl.ds(3 * g + 2, 1), columns],
+                gain,
+                s.cosine[:, columns],
+                s.sine[:, columns],
+            )
+            s.t_qkv[pl.ds(512 * g + 256, 128), columns] = grad.astype(BF16)
             s.gain_k_sum[...] += gain_part
-            s.t_qkv[pl.ds(768 + 128 * g, 128), columns] = s.keep_own[columns, pl.ds(128 * g, 128)].T.astype(BF16)
-
-    loop(4, key_back)
-
-    def in_back(b, store):
+            s.t_qkv[pl.ds(512 * g + 384, 128), columns] = s.keep_own[columns, pl.ds(128 * g, 128)].T.astype(BF16)
+
+        loop(4, body)
+
+    def tell_ready(g):
+        for k, name in enumerate(PARTNERS[2:]):
+            pl.semaphore_signal(ready.at[g, k], inc=1, device_id=place.device(name), device_id_type=MESH)
+
+    def wait_ready(g):
+        for k in range(5):
+            pl.semaphore_wait(ready.at[g, k], 1)
+
+    def qkv_grad(g):
         def body(i):
-            store(i, nn(s.w_qkv[span(i), :], s.t_qkv[:, span(b)]))
+            values = nt(s.h1[span(i), :], s.t_qkv[pl.ds(512 * g, 512), :]).astype(BF16)
+            s.attn_mix[i, :, :, pl.ds(512 * g, 512)] = values.reshape(4, 64, 512)
 
         loop(4, body)
+
+    def out_grad(i):
+        s.attn_mix[i, :, :, pl.ds(1024, 512)] = nt(s.da[span(i), :], s.ob[...]).astype(BF16).reshape(4, 64, 512)
+
+    gather_da.near_ready()
+    loop(2, lambda i: out_back(place.far * 2 + i))
+    for g in range(2):
+        loop(2, lambda i, g=g: attend_back(place.far * 2 + i, g))
+    gather_da.pass_on()
+    for half in range(2):
+        sum_mlp.send_far(half)
+    dp_mlp.advance()
+    gather_da.far_ready()
+    loop(2, lambda i: out_back((1 - place.far) * 2 + i))
+    gather_dy.drain()
+
+    loop(2, lambda i: attend_back((1 - place.far) * 2 + i, 1))
+    dp_mlp.advance()
+    key_back(1)
+    tell_ready(1)
+    loop(4, out_grad)
+    qkv_grad(1)
+    wait_ready(1)
+    dp_high = DpSum(links, s.attn_mix, 512, HIGH_STREAMS, s.p, s.sums, 512)
+    dp_high.advance()
+    loop(2, lambda i: attend_back((1 - place.far) * 2 + i, 0))
+    dp_mlp.advance()
+    key_back(0)
+    tell_ready(0)
+
+    def in_back(b, store, first=0, last=4):
+        columns = span(b)
+
+        def body(i):
+            values = nn(s.w_qkv[span(i), :], s.t_qkv[:, columns])
+            product = values * s.h1[span(i), columns].astype(F32)
+            s.gain_sum[span(i), :] += product[:, :128] + product[:, 128:]
+            store(i, values)
+
+        lax.fori_loop(first, last, lambda i, carry: (body(i), carry)[1], 0)
 
     sum_dh1 = Reduce(links, s.sib_out, s.sib_in, s.far_out, s.far_in)
     in_back(across_sib, to(s.sib_out, 0))
     sum_dh1.to_sibling(0)
-    in_back(across, to(s.keep_far))
     for half in range(2):
+        in_back(across, to(s.keep_far), 2 * half, 2 * half + 2)
         sum_dh1.make_far(s.keep_far, half)
         sum_dh1.send_far(half)
-    gather_dy.drain()
-
-    def qkv_grad(i):
-        for j in range(2):
-            values = nt(s.h1[span(i), :], s.t_qkv[pl.ds(512 * j, 512), :]).astype(BF16)
-            s.attn_mix[i, :, :, pl.ds(512 * j, 512)] = values.reshape(4, 64, 512)
-
-    loop(4, qkv_grad)
-    for k in range(5):
-        pl.semaphore_wait(ready.at[k], 1)
-    dp_mlp.advance()
-    dp_attn = DpSum(links, s.attn_mix, ATTN_WIDTHS, s.p, s.sums, 0)
-    dp_attn.advance()
+    qkv_grad(0)
+    wait_ready(0)
+    dp_low = DpSum(links, s.attn_mix, 0, LOW_STREAMS, s.p, s.sums, 0)
+    dp_low.advance()
+    dp_high.advance()
     in_back(sib, to(s.sib_out, 1))
     sum_dh1.to_sibling(1)
     in_back(me, to(s.keep_own))
+    s.gain_parts[0, 0:1, :] = jnp.sum((s.gain_sum[...] / s.gain1[...]).T, axis=0, keepdims=True)
     for row, part in ((0, s.gain_q_sum), (1, s.gain_k_sum)):
         both = part[:, pl.ds(0, 128)] + part[:, pl.ds(128, 128)]
         s.gain_parts[0, 2:3, pl.ds(128 * row, 128)] = jnp.sum(both.T, axis=0, keepdims=True)
     s.gain_parts[0, 2:3, pl.ds(256, 768)] = jnp.zeros((1, 768), F32)
     s.gain_parts[0, pl.ds(3, 5), :] = jnp.zeros((5, 1024), F32)
+    gains = GainSum(links, s.gain_parts)
+    dp_low.advance()
+    dp_high.advance()
+    dp_mlp.advance()
+    gains.advance()
 
     sum_mlp.arrive()
 
     def layer_out(i):
-        out[:, span(i)] = sum_mlp.total(s.mlp_own, span(i)).T.astype(BF16)
+        s.stage[:, span(i)] = sum_mlp.total(s.mlp_own, span(i)).T.astype(BF16)
 
     loop(4, layer_out)
-    dp_attn.advance()
+    load(s.stage, out)
+    dp_low.advance()
+    dp_high.advance()
+    dp_mlp.advance()
+    gains.advance()
 
     sum_dh1.arrive()
 
@@ -801,48 +893,60 @@
         grad = sum_dh1.total(s.keep_own, rows)
         s.keep_own[rows, :] = grad
         product = grad * (s.x_t[rows, :].astype(F32) * s.root1[0:1])
-        s.gain_sum[rows, :] = product[:, :128] + product[:, 128:]
         return total + fold(product * twice(s.gain1[rows, :]))
 
     inner = lax.fori_loop(0, 8, last_back_sum, jnp.zeros((8, BLOCK), F32))
     inner = jnp.sum(inner, axis=0, keepdims=True) / 1024.0
-    s.gain_parts[0, 0:1, :] = jnp.sum(s.gain_sum[...].T, axis=0, keepdims=True)
-    gain_copies = [links.send(s.gain_parts.at[0], s.gain_parts.at[7], GAIN_ORDER[0])]
 
     def last_back(i):
         rows = span(i)
         scaled = s.keep_own[rows, :] * twice(s.gain1[rows, :])
         normed = s.x_t[rows, :].astype(F32) * s.root1[0:1]
-        grad_x[:, rows] = (s.resid[rows, :] + s.root1[0:1] * (scaled - normed * inner)).T
+        s.result[:, rows] = (s.resid[rows, :] + s.root1[0:1] * (scaled - normed * inner)).T
 
     loop(4, last_back)
-
-    for step in range(7):
-        if step % 2 == 0 and dp_attn.phase < 5:
-            dp_attn.advance()
-        gain_copies[step].wait_recv()
-        total = s.gain_parts[step] + s.gain_parts[7 + step]
-        if step < 6:
-            s.gain_parts[step + 1] = total
-            following = links.send(s.gain_parts.at[step + 1], s.gain_parts.at[8 + step], GAIN_ORDER[step + 1])
-            gain_copies.append(following)
-        else:
-            out_g1[...] = total[0:1]
-            out_g2[...] = total[1:2]
-            out_gq[...] = total[2:3, :128]
-            out_gk[...] = total[2:3, 128:256]
-    out_q[...] = s.sums[:, pl.ds(0, 512)]
-    out_k[...] = s.sums[:, pl.ds(512, 256)]
-    out_v[...] = s.sums[:, pl.ds(768, 256)]
-    out_o[...] = s.sums[:, pl.ds(1024, 512)].T
-    out_g[...] = s.sums[:, pl.ds(1536, 768)]
-    out_u[...] = s.sums[:, pl.ds(2304, 768)]
-    out_d[...] = s.sums[:, pl.ds(3072, 768)].T
-
-    for copy in gain_copies:
-        copy.wait_send()
-    for exchange in (gather_h1, gather_da, sum_mlp, sum_dh1, dp_mlp, dp_attn):
+    load(s.result, grad_x)
+    dp_mlp.complete()
+    while dp_low.phase < 5 or dp_high.phase < 5 or gains.step < 7:
+        dp_low.advance()
+        dp_high.advance()
+        gains.advance()
+    load(s.sums, out_sums)
+    out_g1[...] = gains.total[0:1]
+    out_g2[...] = gains.total[1:2]
+    out_gq[...] = gains.total[2:3, :128]
+    out_gk[...] = gains.total[2:3, 128:256]
+
+    for copy in loads[12:]:
+        copy.wait()
+    for exchange in (gather_h1, gather_da, sum_mlp, sum_dh1, dp_mlp, dp_high, dp_low, gains):
         exchange.drain()
+
+
+def deliver_kernel(*refs):
+    given, outs, held, (sems_in, sems_out) = refs[:7], refs[7:20], refs[20:27], refs[27:]
+    copies = [pltpu.make_async_copy(a, b, sems_in.at[k]) for k, (a, b) in enumerate(zip(given, held))]
+    for copy in copies:
+        copy.start()
+    sums = held[2]
+    parts = [(held[0], outs[0]), (held[1], outs[1])]
+    for g in range(2):
+        for out, first, width in ((outs[2], 0, 256), (outs[3], 256, 128), (outs[4], 384, 128)):
+            parts.append((sums.at[:, pl.ds(512 * g + first, width)], out.at[:, pl.ds(width * g, width)]))
+    for out, first, width in ((outs[5], 1024, 512), (outs[6], 1536, 768), (outs[7], 2304, 768), (outs[8], 3072, 768)):
+        parts.append((sums.at[:, pl.ds(first, width)], out))
+    parts += list(zip(held[3:], outs[9:]))
+    arrived = [False] * 7
+    started = []
+    for k, (src, dst) in enumerate(parts):
+        need = k if k < 2 else 2 if k < 12 else k - 9
+        if not arrived[need]:
+            copies[need].wait()
+            arrived[need] = True
+        started.append(pltpu.make_async_copy(src, dst, sems_out.at[k]))
+        started[k].start()
+    for copy in started:
+        copy.wait()
 
 
 def shards(
@@ -870,30 +974,19 @@
     def shaped(*shape, kind=F32):
         return jax.ShapeDtypeStruct(shape, kind)
 
+    gains = (shaped(1, 1024), shaped(1, 1024), shaped(1, 128), shaped(1, 128))
+    given = (shaped(256, 1024, kind=BF16), shaped(256, 1024), shaped(32, 3840), *gains)
+    widths = (512, 256, 256, 512, 768, 768, 768)
     outs = pl.pallas_call(
         layer_kernel,
-        out_shape=(
-            shaped(256, 1024, kind=BF16),
-            shaped(256, 1024),
-            shaped(32, 512),
-            shaped(32, 256),
-            shaped(32, 256),
-            shaped(512, 32),
-            shaped(32, 768),
-            shaped(32, 768),
-            shaped(768, 32),
-            shaped(1, 1024),
-            shaped(1, 1024),
-            shaped(1, 128),
-            shaped(1, 128),
-        ),
-        in_specs=[vmem, smem, vmem] + [hbm] * 7 + [vmem] * 5,
-        out_specs=(vmem,) * 13,
+        out_shape=given,
+        in_specs=[vmem, smem] + [hbm] * 8 + [vmem] * 5,
+        out_specs=(hbm,) * 3 + (vmem,) * 4,
         scratch_shapes=[pltpu.VMEM(shape, kind) for _, shape, kind in SCRATCH]
         + [
             pltpu.SemaphoreType.DMA((2, SEMAPHORES)),
-            pltpu.SemaphoreType.DMA((8,)),
-            pltpu.SemaphoreType.REGULAR((5,)),
+            pltpu.SemaphoreType.DMA((16,)),
+            pltpu.SemaphoreType.REGULAR((2, 5)),
         ],
         compiler_params=pltpu.CompilerParams(
             collective_id=0, has_side_effects=True, vmem_limit_bytes=64 * 2**20 - 2**16
@@ -917,10 +1010,22 @@
         gain_key.reshape(1, 128),
         frequency,
     )
+    outs = pl.pallas_call(
+        deliver_kernel,
+        out_shape=given[:2] + tuple(shaped(32, width) for width in widths) + gains,
+        in_specs=[hbm] * 7,
+        out_specs=(hbm,) * 13,
+        scratch_shapes=[pltpu.VMEM(one.shape, one.dtype) for one in given]
+        + [pltpu.SemaphoreType.DMA((7,)), pltpu.SemaphoreType.DMA((16,))],
+        name="deliver",
+    )(*outs)
     return (
         outs[0].reshape(1, 256, 1024),
         outs[1].reshape(1, 256, 1024),
-        *outs[2:9],
+        *outs[2:5],
+        outs[5].T,
+        *outs[6:8],
+        outs[8].T,
         *(gain.reshape(-1) for gain in outs[9:]),
     )
 

time: 178 us -> 155 us (0.87)
  local copies, waits for them, and re-layouts: 11.8 us -> 0 us
  Pallas kernels: 165 us -> 154 us
    unnamed x33 -> x0, local copies, waits for them, and re-layouts: 11.8 us -> none
    pallas_call x1 -> x2, Pallas kernels: 165 us -> 154 us  [the longest x1 151 us: shards(): pl.pallas_call(layer_kernel, out_shape=given, in_specs=[vmem, smem] + [hb...]
where the time goes in v3:
time: 155 us
  Pallas kernels  154 us (99%)
    pallas_call x1, Pallas kernels, shards(): pl.pallas_call(layer_kernel, out_shape=given, in_specs=[vmem, smem] + [hb...  151 us

profile of v3, /device:TPU:6, one launch (start us, length us, event | category | flops | bytes accessed | tf_op | source)
XLA Modules:
  0.0 154.6 jit_solution(16891127598558383509)
XLA Ops:
  0.7 151.1 %layer.1 = (bf16[256,1024]{1,0:T(8,128)(2,1)}, f32[256,1024]{1,0:T(8,128)}, f32[32,3840]{1,0:T(8,128)}, f32[1,1024]{1,0:T(1,128)}, f32[1,1024]{1,0:T(1,128)}, /*index=5*/f32[1,128]{1,0:T(1,128)}, f32[1,128]{1,0:T(1,128)}) custom-call(bf16[256,1024]{1,0:T(8,128)(2,1)} %bitcast.19, s32[1,4]{1,0:T(1,128)} %starts.1, bf16[256,1024]{1,0:T(8,128)(2,1)} %bitcast.20, ...), custom_call_target="tpu_custom_call" | custom-call | flops 32000000000 | bytes 16777216 | tf_op jit(solution)/shard_map/layer/pallas_call | solution.py:980
  151.8 2.7 %deliver.1 = (bf16[256,1024]{1,0:T(8,128)(2,1)}, f32[256,1024]{1,0:T(8,128)}, f32[32,512]{1,0:T(8,128)}, f32[32,256]{1,0:T(8,128)}, f32[32,256]{1,0:T(8,128)}, /...) custom-call(bf16[256,1024]{1,0:T(8,128)(2,1)} %get-tuple-element.33., ...), custom_call_target="tpu_custom_call" | custom-call | tf_op jit(solution)/shard_map/deliver/pallas_call | solution.py:1013
